TPU v7x, 256 devices: a whole 4x4x8 slice. The times are simulated.
256 devices in a mesh: bin: 16 (over z_lo, x), coil: 16 (over y, z_hi, core).
Axes of the slice: x: 4, y: 4, z: 8 (z_hi: 2, z_lo: 4; z = z_hi * 4 + z_lo), core: 2. Of those that a mesh axis runs over, the one named last changes fastest.
Arguments:
- kspace: float32 [32, 32, 4, 2, 96, 256], P('bin', 'coil'), may hold values from -6 to 6
- coil_maps: float32 [32, 4, 2, 96, 256], P('coil'), may hold values from -1 to 1
- sample_mask: int32 [32, 96, 256], P('bin'), may hold values from 0 to 1, as said below
Outputs:
- image: float32 [32, 4, 2, 96, 256], P('bin')
Inputs may be any that keep to these rules, and one draw needn't show every extreme that they name: `sample_mask`: 0/1 entries; the share of sampled lines differs from bin to bin.
All inputs are finite; a program needn't handle non-finite values.
Results may differ from a plain program's by a relative error of at most 0.0015.
Values sent between devices are 32-bit elements; how exact they have to be, the bound alone decides.
A program may use at most 64 MiB of HBM per device.

v0:
```python
import math

import jax
import jax.numpy as jnp
from jax import lax
from jax.sharding import PartitionSpec as P

ITERS = 2


highest = lax.Precision.HIGHEST


def passed_along(value, axis, steps):
    count = lax.axis_size(axis)
    initial, last = (max(0, -steps), min(count, count - steps))
    return lax.ppermute(value, axis, [(source, source + steps) for source in range(initial, last)])


def dft_tables(length):
    index = jnp.arange(length, dtype=jnp.int32)
    turns = index[:, None] * index[None, :] % length
    angle = turns.astype(jnp.float32) * (2.0 * math.pi / length)
    factor = 1.0 / math.sqrt(length)
    return (jnp.cos(angle) * factor, jnp.sin(angle) * factor)


def along_rows(values, table):
    return jnp.einsum("...y,yk->...k", values, table, precision=highest)


def along_cols(table, values):
    return jnp.einsum("kz,...zy->...ky", table, values, precision=highest)


def transform(real_part, imag_part, tables, sign):
    cos_z, sin_z, cos_y, sin_y = tables
    mid_re = along_rows(real_part, cos_y) + sign * along_rows(imag_part, sin_y)
    mid_im = along_rows(imag_part, cos_y) - sign * along_rows(real_part, sin_y)
    out_re = along_cols(cos_z, mid_re) + sign * along_cols(sin_z, mid_im)
    out_im = along_cols(cos_z, mid_im) - sign * along_cols(sin_z, mid_re)
    return (out_re, out_im)


def combine_coils(wave_re, wave_im, coil_maps):
    sens_re = coil_maps[None, :, :, 0]
    sens_im = coil_maps[None, :, :, 1]
    total_re = jnp.sum(sens_re * wave_re + sens_im * wave_im, axis=1)
    total_im = jnp.sum(sens_re * wave_im - sens_im * wave_re, axis=1)
    return jnp.stack([total_re, total_im], axis=2)


def adjoint_terms(kspace, coil_maps, weights, tables):
    wave_re, wave_im = transform(
        kspace[:, :, :, 0] * weights, kspace[:, :, :, 1] * weights, tables, -1.0
    )
    return combine_coils(wave_re, wave_im, coil_maps)


def normal_terms(field, coil_maps, weights, tables):
    sens_re = coil_maps[None, :, :, 0]
    sens_im = coil_maps[None, :, :, 1]
    field_re = field[:, None, :, 0]
    field_im = field[:, None, :, 1]
    coil_re = sens_re * field_re - sens_im * field_im
    coil_im = sens_re * field_im + sens_im * field_re
    spec_re, spec_im = transform(coil_re, coil_im, tables, 1.0)
    wave_re, wave_im = transform(spec_re * weights, spec_im * weights, tables, -1.0)
    return combine_coils(wave_re, wave_im, coil_maps)


def on_device(kspace, coil_maps, sample_mask):
    cos_z, sin_z = dft_tables(kspace.shape[4])
    cos_y, sin_y = dft_tables(kspace.shape[5])
    tables = (cos_z, sin_z, cos_y, sin_y)
    weights = sample_mask.astype(jnp.float32)[:, None, None]

    def reduce_coils(terms):
        return lax.psum(terms, "coil")

    def inner(value):
        return lax.psum(value, "bin")

    rhs = reduce_coils(adjoint_terms(kspace, coil_maps, weights, tables))
    solution = jnp.zeros_like(rhs)
    resid = rhs
    direction = rhs
    norm_now = inner(jnp.sum(resid * resid))
    for step in range(ITERS):
        full_dir = direction
        image_dir = (
            reduce_coils(normal_terms(full_dir, coil_maps, weights, tables)) + 0.1 * direction
        )
        alpha = norm_now / inner(jnp.sum(direction * image_dir))
        solution = solution + alpha * direction
        if step + 1 < ITERS:
            resid = resid - alpha * image_dir
            norm_next = inner(jnp.sum(resid * resid))
            direction = resid + norm_next / norm_now * direction
            norm_now = norm_next
    bins_here = solution.shape[0]
    total_bins = bins_here * lax.axis_size("bin")
    first_bin = lax.axis_index("bin") * bins_here
    count = (total_bins - 1) * solution.shape[1] * solution.shape[3] * solution.shape[4]
    upper = passed_along(solution[:1], "bin", -1)
    after = jnp.concatenate([solution[1:], upper], axis=0)
    bin_ids = first_bin + jnp.arange(bins_here, dtype=jnp.int32)
    keep = (bin_ids < total_bins - 1).astype(jnp.float32)[:, None, None, None, None]
    diff = (after - solution) * keep
    magnitude = jnp.sqrt(diff[:, :, 0] * diff[:, :, 0] + diff[:, :, 1] * diff[:, :, 1])
    partial_sum = jnp.sum(magnitude)
    scale_sum = lax.psum(partial_sum, "bin")
    lam = 1.0 * scale_sum / count + 1e-06
    dual = diff * (lam / jnp.maximum(magnitude, lam))[:, :, None]
    before = passed_along(dual[-1:], "bin", 1)
    prior = jnp.concatenate([before, dual[:-1]], axis=0)
    return solution + 0.25 * (dual - prior)


def solution(mesh):
    return jax.shard_map(
        on_device,
        mesh=mesh,
        in_specs=(
            P("bin", "coil", None, None, None, None),
            P("coil", None, None, None, None),
            P("bin", None, None),
        ),
        out_specs=P("bin", None, None, None, None),
        check_vma=False,
    )
```

profile of v0, /device:TPU:2, one launch (start us, length us, event | category | flops | bytes accessed | tf_op | source)
XLA Modules:
  0.0 879.2 jit_solution(1652024554082887885)
XLA Ops:
  7.5 4.0 fusion.28
  11.5 2.4 fusion.27
  13.9 2.5 multiply_subtract_fusion.12
  18.1 2.5 multiply_add_fusion.14
  28.2 189.4 %all-reduce.5.cloned.1.call-done = f32[2,4,2,96,256]{4,3,2,1,0:T(8,128)} async-done(((f32[2,4,2,96,256]{4,3,2,1,0:T(8,128)}), f32[2,4,2,96,256]{4,3,2,1,0:T(8,128)}) %all-reduce.5.cloned.1.call-update) | async-done | bytes 1572880 | tf_op jit(solution)/shard_map/psum | solution.py:79
  219.2 2.6 fusion.20
  221.7 2.5 fusion.19
  224.3 2.6 fusion.23
  228.6 2.6 fusion.24
  236.7 2.4 fusion.86
  239.1 2.4 fusion.88
  241.5 2.7 multiply_subtract_fusion.7
  244.2 2.5 multiply_add_fusion.9
  255.5 187.6 %all-reduce.7.cloned.1.call-done = f32[2,4,2,96,256]{4,3,2,1,0:T(8,128)} async-done(((f32[2,4,2,96,256]{4,3,2,1,0:T(8,128)}), f32[2,4,2,96,256]{4,3,2,1,0:T(8,128)}) %all-reduce.7.cloned.1.call-update) | async-done | bytes 1572880 | tf_op jit(solution)/shard_map/psum | solution.py:79
  443.2 2.5 multiply_reduce_fusion.2
  445.6 38.7 %all-reduce = (f32[]{:T(128)}, f32[]{:T(128)}) all-reduce(f32[]{:T(128)} %get-tuple-element.12, f32[]{:T(128)} %get-tuple-element.11), channel_id=1, replica_groups=mesh['bin'=16,'coil'=16] {'bin'}, use_global_device_ids=true, to_apply=%region_4.5 | all-reduce | flops 2 | bytes 16 | tf_op jit(solution)/shard_map/psum | solution.py:82
  485.6 2.4 multiply_reduce_fusion.1
  488.0 42.5 %psum.60 = f32[]{:T(128)} all-reduce(f32[]{:T(128)} %multiply_reduce_fusion.1), channel_id=1, replica_groups=mesh['bin'=16,'coil'=16] {'bin'}, use_global_device_ids=true, to_apply=%region_11.12 | all-reduce | flops 1 | bytes 8 | tf_op jit(solution)/shard_map/psum | solution.py:82
  534.6 2.5 fusion.16
  537.1 2.5 fusion.15
  539.7 2.6 fusion.25
  544.0 2.8 fusion.26
  552.1 2.4 fusion.80
  556.9 2.7 multiply_subtract_fusion.1
  559.6 2.5 multiply_add_fusion.2
  570.9 178.4 %all-reduce.9.cloned.1.call-done = f32[2,4,2,96,256]{4,3,2,1,0:T(8,128)} async-done(((f32[2,4,2,96,256]{4,3,2,1,0:T(8,128)}), f32[2,4,2,96,256]{4,3,2,1,0:T(8,128)}) %all-reduce.9.cloned.1.call-update) | async-done | bytes 1572880 | tf_op jit(solution)/shard_map/psum | solution.py:79
  749.3 2.4 multiply_reduce_fusion
  751.7 38.7 %psum.62 = f32[]{:T(128)} all-reduce(f32[]{:T(128)} %multiply_reduce_fusion), channel_id=1, replica_groups=mesh['bin'=16,'coil'=16] {'bin'}, use_global_device_ids=true, to_apply=%region_16.17 | all-reduce | flops 1 | bytes 8 | tf_op jit(solution)/shard_map/psum | solution.py:82
  794.2 6.0 collective-permute-start
  800.2 9.6 %collective-permute-done = f32[1,4,2,96,256]{4,3,2,1,0:T(8,128)S(1)} collective-permute-done((f32[1,4,2,96,256]{4,3,2,1,0:T(8,128)S(1)}, f32[1,4,2,96,256]{4,3,2,1,0:T(8,128)S(1)}, u32[]{:S(2)}, u32[]{:S(2)}) %collective-permute-start) | collective-permute-done | bytes 786464 | tf_op jit(solution)/shard_map/ppermute | solution.py:17
  813.3 41.0 %psum.63 = f32[]{:T(128)} all-reduce(f32[]{:T(128)} %fusion.97), channel_id=1, replica_groups=mesh['bin'=16,'coil'=16] {'bin'}, use_global_device_ids=true, to_apply=%region_18.19 | all-reduce | flops 1 | bytes 8 | tf_op jit(solution)/shard_map/psum | solution.py:112
  858.7 12.0 %collective-permute-done.1 = f32[1,4,2,96,256]{4,3,2,1,0:T(8,128)S(1)} collective-permute-done((f32[1,4,2,96,256]{4,3,2,1,0:T(8,128)S(1)}, f32[1,4,2,96,256]{4,3,2,1,0:T(8,128)S(1)}, u32[]{:S(2)}, u32[]{:S(2)}) %collective-permute-start.1) | collective-permute-done | bytes 786464 | tf_op jit(solution)/shard_map/ppermute | solution.py:17
  (61 shorter events, 60.5 us)
Async XLA Ops:
  6.5 211.1 %all-reduce.5.cloned.1.call-start = ((), (), s32[]{:S(2)}) async-start(), calls=%async_computation | async-start | bytes 3145728 | tf_op jit(solution)/shard_map/psum | solution.py:79
  7.5 4.0 copy-start.3
  22.6 1.8 copy-start.7
  28.2 415.0 %all-reduce.7.cloned.1.call-start = ((), (), s32[]{:S(2)}) async-start(), calls=%async_computation.1 | async-start | bytes 3145728 | tf_op jit(solution)/shard_map/psum | solution.py:79
  255.5 187.7 %copy-start = (f32[2,4,2,96,256]{4,3,2,1,0:T(8,128)S(1)}, f32[2,4,2,96,256]{4,3,2,1,0:T(8,128)}, u32[]{:S(2)}) copy-start(f32[2,4,2,96,256]{4,3,2,1,0:T(8,128)} %all-reduce.5.cloned.1.call-done) | copy-start | bytes 4718596
  255.5 493.8 %all-reduce.9.cloned.1.call-start = ((), (), s32[]{:S(2)}) async-start(), calls=%async_computation.2 | async-start | bytes 3145728 | tf_op jit(solution)/shard_map/psum | solution.py:79
  533.4 1.1 copy-start.1
  570.9 178.4 %copy-start.2 = (f32[2,4,2,96,256]{4,3,2,1,0:T(8,128)S(1)}, f32[2,4,2,96,256]{4,3,2,1,0:T(8,128)}, u32[]{:S(2)}) copy-start(f32[2,4,2,96,256]{4,3,2,1,0:T(8,128)} %copy-done.1) | copy-start | bytes 4718596
  794.2 15.6 %collective-permute-start = (f32[1,4,2,96,256]{4,3,2,1,0:T(8,128)S(1)}, f32[1,4,2,96,256]{4,3,2,1,0:T(8,128)S(1)}, u32[]{:S(2)}, u32[]{:S(2)}) collective-permute-start(f32[1,4,2,96,256]{4,3,2,1,0:T(8,128)S(1)} %get-tuple-element.18), channel_id=1, source_target_pairs={{16,0},{32,16},{48,32},{64,48},{80,64},{96,80},{112,96},{128,112},... | collective-permute-start | bytes 2359304 | tf_op jit(solution)/shard_map/ppermute | solution.py:17
  809.8 0.9 copy-start.5
  854.9 1.1 copy-start.4
  854.9 1.4 copy-start.6
  856.8 13.9 %collective-permute-start.1 = (f32[1,4,2,96,256]{4,3,2,1,0:T(8,128)S(1)}, f32[1,4,2,96,256]{4,3,2,1,0:T(8,128)S(1)}, u32[]{:S(2)}, u32[]{:S(2)}) collective-permute-start(f32[1,4,2,96,256]{4,3,2,1,0:T(8,128)S(1)} %get-tuple-element.15), channel_id=1, source_target_pairs={{0,16},{16,32},{32,48},{48,64},{64,80},{80,96},{96,112},{112,128},... | collective-permute-start | bytes 2359304 | tf_op jit(solution)/shard_map/ppermute | solution.py:17
Sparse Core Ops, SparseCore 0:
  28.3 189.2 all-reduce.4
  255.6 187.4 all-reduce.6
  571.0 178.1 all-reduce.8
where the time goes:
time: 888 us; the launch traced here: 879 us
  waiting for transfers between devices  577 us (65%)
  blocking collectives  161 us (18%)
  matrix products  89 us (10%)
  other arithmetic  20.4 us (2%)
  between operations  18.3 us (2%)
    psum x3, waiting for transfers between devices, reduce_coils(): return lax.psum(terms, 'coil')  555 us
    psum x3, blocking collectives, inner(): return lax.psum(value, 'bin')  120 us
    dot_general x20, matrix products, along_rows(): return jnp.einsum('...y,yk->...k', values, table, precision=highest)  51.9 us
    psum x1, blocking collectives, on_device(): scale_sum = lax.psum(partial_sum, 'bin')  41 us
    dot_general x20, matrix products, along_cols(): return jnp.einsum('kz,...zy->...ky', table, values, precision=highest)  37.2 us
    ppermute x2, waiting for transfers between devices, passed_along(): lax.ppermute(value, axis, [(source, source + steps) for source in range(i...  21.5 us
  transfers between devices with their start and end apart: 5, of which 5 were waited for; matrix products, arithmetic and copies ran while one was open for 0% of the time, Pallas kernels for 0%

commit v1 on v0

v1 whole, which is shorter than its diff:
```python
import math

import jax
import jax.numpy as jnp
import numpy as np
from jax import lax
from jax.experimental import pallas as pl
from jax.experimental.pallas import tpu as pltpu
from jax.sharding import PartitionSpec as P

MESH = pl.DeviceIdType.MESH
F32 = jnp.float32
BF16 = jnp.bfloat16
NZ, NY, SL = 96, 256, 4
BIN_AXIS, COIL_AXIS = 16, 16
BINS = 32
COUNT = (BINS - 1) * SL * NZ * NY
PLANE = (2, NZ, NY)


def dft_tables(length):
    index = np.arange(length)
    angle = (index[:, None] * index[None, :] % length) * (2.0 * math.pi / length)
    factor = 1.0 / math.sqrt(length)
    return np.cos(angle) * factor, np.sin(angle) * factor


def halves(table):
    high = table.astype(np.float32).astype(jnp.bfloat16)
    low = (table - high.astype(np.float64)).astype(np.float32).astype(jnp.bfloat16)
    return np.stack([high, low])


def row_tables():
    cos, sin = dft_tables(NY)
    forward = np.block([[cos, -sin], [sin, cos]])
    return np.stack([halves(forward), halves(forward.T)])


def col_tables():
    cos, sin = dft_tables(NZ)
    forward = np.block([[cos, sin], [-sin, cos]])
    return np.stack([halves(forward), halves(forward.T)])


def split(values):
    high = values.astype(BF16)
    return high, (values - high.astype(F32)).astype(BF16)


def dot(left, right):
    return jnp.dot(left, right, preferred_element_type=F32)


def rows(high, low, table, which):
    return dot(high, table[which, 0]) + dot(low, table[which, 0]) + dot(high, table[which, 1])


def cols(values, table, which):
    high, low = split(values)
    return dot(table[which, 0], high) + dot(table[which, 0], low) + dot(table[which, 1], high)


def fold(values):
    part = jnp.sum(values.reshape(values.shape[0] // 8, 8, NY), axis=0)
    return part[:, :128] + part[:, 128:]


def total(values):
    return jnp.sum(values, keepdims=True)


def kernel(
    kspace, coil_maps, mask, row_table, col_table, out,
    maps, weight, high, low, mid, part, from_sib, to_y, from_y, to_z, from_z,
    rhs, quad, resid, image, near_rhs, near_resid, message, sums,
    map_send, map_recv, map_sib_send, map_sib_recv, map_local,
    sib_send, sib_recv, y_send, y_recv, z_send, z_recv,
    near_send, near_recv, sum_send, sum_recv,
    out_send, out_recv, out_sib_send, out_sib_recv, out_local,
):
    b = lax.axis_index("bin")
    j = lax.axis_index("coil")
    y, z, c = j // 4, (j // 2) % 2, j % 2

    def at_y(step):
        return (b, lax.rem(y + step, 4) * 4 + z * 2 + c)

    sibling = (b, j + 1 - 2 * c)
    opposite = (b, j + 2 - 4 * z)
    across = (lax.rem(b + 2 * c - 1 + BIN_AXIS, BIN_AXIS), j + 1 - 2 * c)

    def send(source, target, send_sem, recv_sem, device):
        copy = pltpu.make_async_remote_copy(
            src_ref=source, dst_ref=target, send_sem=send_sem, recv_sem=recv_sem,
            device_id=device, device_id_type=MESH,
        )
        copy.start()
        return copy

    barrier = pltpu.get_barrier_semaphore()
    for step in range(1, COIL_AXIS):
        pl.semaphore_signal(barrier, inc=1, device_id=(b, lax.rem(j + step, COIL_AXIS)), device_id_type=MESH)
    for step in range(1, BIN_AXIS):
        pl.semaphore_signal(barrier, inc=1, device_id=(lax.rem(b + step, BIN_AXIS), j), device_id_type=MESH)
    pl.semaphore_signal(barrier, inc=1, device_id=across, device_id_type=MESH)
    pl.semaphore_wait(barrier, COIL_AXIS + BIN_AXIS - 1)

    own_maps = pltpu.make_async_copy(coil_maps.at[:, y], maps.at[0, c], map_local)
    own_maps.start()
    map_copies = [
        send(coil_maps.at[:, lax.rem(y + step, 4)], maps.at[4 - step, c],
             map_send.at[step - 1], map_recv.at[4 - step - 1], at_y(step))
        for step in (1, 2, 3)
    ]
    sib_maps = [send(coil_maps.at[:, y], maps.at[0, c], map_sib_send.at[0], map_sib_recv.at[0], sibling)]

    weight[0] = mask[0].astype(F32)
    weight[1] = mask[1].astype(F32)

    def sib_copy(k):
        return pltpu.make_async_remote_copy(
            src_ref=part.at[k, 1 - c], dst_ref=from_sib.at[k],
            send_sem=sib_send.at[k], recv_sem=sib_recv.at[k],
            device_id=sibling, device_id_type=MESH,
        )

    def y_copy(k):
        return pltpu.make_async_remote_copy(
            src_ref=to_y.at[k], dst_ref=from_y.at[k],
            send_sem=y_send.at[k], recv_sem=y_recv.at[k],
            device_id=at_y(3 - k), device_id_type=MESH,
        )

    def adjoint(k, carry):
        s = lax.rem(y + 3 - k, 4)
        for t in range(4):
            w = weight[t // 2]
            values = jnp.concatenate(
                [kspace[t // 2, t % 2, s, 0] * w, kspace[t // 2, t % 2, s, 1] * w], axis=1
            )
            high[t * NZ:(t + 1) * NZ], low[t * NZ:(t + 1) * NZ] = split(values)
        mid[...] = rows(high[...], low[...], row_table, 1)
        for bin_ in range(2):
            sum_re, sum_im = 0.0, 0.0
            for coil in range(2):
                at = pl.ds((bin_ * 2 + coil) * NZ, NZ)
                wave = cols(jnp.concatenate([mid[at, :NY], mid[at, NY:]], axis=0), col_table, 1)
                sens_re, sens_im = coil_maps[coil, s, 0], coil_maps[coil, s, 1]
                sum_re += sens_re * wave[:NZ] + sens_im * wave[NZ:]
                sum_im += sens_re * wave[NZ:] - sens_im * wave[:NZ]
            part[k, bin_, 0] = sum_re
            part[k, bin_, 1] = sum_im
        sib_copy(k).start()

        @pl.when(k > 0)
        def _():
            sib_copy(k - 1).wait_recv()
            to_y[k - 1] = part[k - 1, c] + from_sib[k - 1]
            y_copy(k - 1).start()

        return carry

    lax.fori_loop(0, 4, adjoint, 0)
    sib_copy(3).wait_recv()
    own = part[3, c] + from_sib[3]
    for k in range(3):
        y_copy(k).wait_recv()
        own = own + from_y[k]
    to_z[0] = own
    z_copy = send(to_z.at[0], from_z.at[0], z_send.at[0], z_recv.at[0], opposite)
    own_maps.wait()
    for slot in (1, 2, 3):
        map_copies[3 - slot].wait_recv()
        sib_maps.append(
            send(maps.at[slot, c], maps.at[slot, c], map_sib_send.at[slot], map_sib_recv.at[slot], sibling)
        )
    z_copy.wait()
    rhs[...] = to_z[0] + from_z[0]
    near = [
        send(rhs, near_rhs.at[0], near_send.at[0], near_recv.at[0], sibling),
        send(rhs, near_rhs.at[1], near_send.at[1], near_recv.at[1], across),
    ]
    for copy in sib_maps:
        copy.wait_recv()

    def spectra(n, field, t):
        sens_re, sens_im = maps[n, t // 2, t % 2, 0], maps[n, t // 2, t % 2, 1]
        values = jnp.concatenate(
            [sens_re * field[0] - sens_im * field[1], sens_re * field[1] + sens_im * field[0]], axis=1
        )
        high[t * NZ:(t + 1) * NZ], low[t * NZ:(t + 1) * NZ] = split(values)

    def masked(t):
        at = pl.ds(t * NZ, NZ)
        values = cols(jnp.concatenate([mid[at, :NY], mid[at, NY:]], axis=0), col_table, 0)
        w = weight[c]
        return values * jnp.concatenate([w, w], axis=0)

    def normal(n, energy):
        for t in range(4):
            spectra(n, rhs, t)
        mid[...] = rows(high[...], low[...], row_table, 0)
        for t in range(4):
            values = masked(t)
            energy = energy + fold(values * values)
            wave = cols(values, col_table, 1)
            wave = jnp.concatenate([wave[:NZ], wave[NZ:]], axis=1)
            high[t * NZ:(t + 1) * NZ], low[t * NZ:(t + 1) * NZ] = split(wave)
        mid[...] = rows(high[...], low[...], row_table, 1)
        sum_re, sum_im = to_z[1, 0], to_z[1, 1]
        for t in range(4):
            at = pl.ds(t * NZ, NZ)
            sens_re, sens_im = maps[n, t // 2, t % 2, 0], maps[n, t // 2, t % 2, 1]
            sum_re += sens_re * mid[at, :NY] + sens_im * mid[at, NY:]
            sum_im += sens_re * mid[at, NY:] - sens_im * mid[at, :NY]
        to_z[1, 0] = sum_re
        to_z[1, 1] = sum_im
        return energy

    def forward(n, energy):
        for t in range(4):
            spectra(n, resid, t)
        mid[...] = rows(high[...], low[...], row_table, 0)
        for t in range(4):
            values = masked(t)
            energy = energy + fold(values * values)
        return energy

    def inner(left, right):
        return fold(left[0] * right[0] + left[1] * right[1])

    def reduce_all(which, parts):
        for n, value in enumerate(parts):
            message[which, 0, n] = value
        for stage in range(2):
            me, size = ((j, COIL_AXIS), (b, BIN_AXIS))[stage]
            used = pl.ds(0, len(parts))
            slots = sums.at[which, stage, :, used]
            copies = []
            for step in range(1, size):
                peer = lax.rem(me + step, size)
                copies.append(
                    send(message.at[which, stage, used], sums.at[which, stage, me, used],
                         sum_send.at[which, stage, step - 1], sum_recv.at[which, stage, step - 1],
                         ((b, peer), (peer, j))[stage])
                )
            sums[which, stage, me, used] = message[which, stage, used]
            for copy in copies:
                copy.wait()
            message[which, stage + 1, used] = jnp.sum(slots[...], axis=0)
        return [total(message[which, 2, n]) for n in range(len(parts))]

    zero = jnp.zeros((8, 128), F32)
    to_z[1] = jnp.zeros(PLANE, F32)
    energy = lax.fori_loop(0, 4, normal, zero)
    z_copy = send(to_z.at[1], from_z.at[1], z_send.at[1], z_recv.at[1], opposite)
    norm_0, energy_0 = reduce_all(0, [0.5 * inner(rhs, rhs), energy])
    curve_0 = energy_0 + 0.1 * norm_0
    alpha_0 = norm_0 / curve_0
    z_copy.wait()
    quad[...] = to_z[1] + from_z[1] + 0.1 * rhs[...]
    resid[...] = rhs[...] - alpha_0 * quad[...]
    near += [
        send(resid, near_resid.at[0], near_send.at[2], near_recv.at[2], sibling),
        send(resid, near_resid.at[1], near_send.at[3], near_recv.at[3], across),
    ]
    energy = lax.fori_loop(0, 4, forward, zero)
    norm_1, cross, energy_1 = reduce_all(
        1, [0.5 * inner(resid, resid), 0.5 * inner(resid, quad), energy]
    )
    beta = norm_1 / norm_0
    curve_1 = energy_1 + 0.1 * norm_1 + 2.0 * beta * cross + beta * beta * curve_0
    alpha_1 = norm_1 / curve_1
    on_rhs = alpha_0 + alpha_1 * beta
    for copy in near:
        copy.wait()
    here = on_rhs * rhs[...] + alpha_1 * resid[...]
    after = on_rhs * near_rhs[c] + alpha_1 * near_resid[c]
    before = on_rhs * near_rhs[1 - c] + alpha_1 * near_resid[1 - c]
    me = 2 * b + c
    diff = jnp.where(me < BINS - 1, after - here, 0.0)
    prior = jnp.where(me > 0, here - before, 0.0)
    size = jnp.sqrt(diff[0] * diff[0] + diff[1] * diff[1])
    prior_size = jnp.sqrt(prior[0] * prior[0] + prior[1] * prior[1])
    (size_sum,) = reduce_all(2, [0.5 * fold(size)])
    lam = size_sum / COUNT + 1e-06
    scale = lam / jnp.maximum(size, lam)
    prior_scale = lam / jnp.maximum(prior_size, lam)
    image[...] = here + 0.25 * (diff * scale[None] - prior * prior_scale[None])

    own_out = pltpu.make_async_copy(image, out.at[c, y], out_local)
    own_out.start()
    copies = [
        send(image, out.at[c, y], out_send.at[step - 1], out_recv.at[4 - step - 1], at_y(step))
        for step in (1, 2, 3)
    ]
    sib_copies = [send(image, out.at[c, y], out_sib_send.at[0], out_sib_recv.at[0], sibling)]
    for slot in (1, 3, 2):
        copies[3 - slot].wait_recv()
        there = out.at[c, lax.rem(y + slot, 4)]
        sib_copies.append(send(there, there, out_sib_send.at[slot], out_sib_recv.at[slot], sibling))
    own_out.wait()
    for k in range(4):
        sib_copy(k).wait_send()
    for k in range(3):
        y_copy(k).wait_send()
        map_copies[k].wait_send()
        copies[k].wait_send()
    for copy in sib_maps:
        copy.wait_send()
    for copy in sib_copies:
        copy.wait()


def on_device(kspace, coil_maps, sample_mask):
    dma = pltpu.SemaphoreType.DMA
    vmem = pl.BlockSpec(memory_space=pltpu.VMEM)
    return pl.pallas_call(
        kernel,
        out_shape=jax.ShapeDtypeStruct((2, SL) + PLANE, F32),
        in_specs=[vmem] * 5,
        out_specs=pl.BlockSpec(memory_space=pl.ANY),
        scratch_shapes=[
            pltpu.VMEM((4, 2, 2) + PLANE, F32),
            pltpu.VMEM(PLANE, F32),
            pltpu.VMEM((4 * NZ, 2 * NY), BF16),
            pltpu.VMEM((4 * NZ, 2 * NY), BF16),
            pltpu.VMEM((4 * NZ, 2 * NY), F32),
            pltpu.VMEM((4, 2) + PLANE, F32),
            pltpu.VMEM((4,) + PLANE, F32),
            pltpu.VMEM((3,) + PLANE, F32),
            pltpu.VMEM((3,) + PLANE, F32),
            pltpu.VMEM((2,) + PLANE, F32),
            pltpu.VMEM((2,) + PLANE, F32),
            pltpu.VMEM(PLANE, F32),
            pltpu.VMEM(PLANE, F32),
            pltpu.VMEM(PLANE, F32),
            pltpu.VMEM(PLANE, F32),
            pltpu.VMEM((2,) + PLANE, F32),
            pltpu.VMEM((2,) + PLANE, F32),
            pltpu.VMEM((3, 3, 3, 8, 128), F32),
            pltpu.VMEM((3, 2, 16, 3, 8, 128), F32),
            dma((3,)), dma((3,)), dma((4,)), dma((4,)), dma(()),
            dma((4,)), dma((4,)), dma((3,)), dma((3,)), dma((2,)), dma((2,)),
            dma((4,)), dma((4,)), dma((3, 2, 15)), dma((3, 2, 15)),
            dma((3,)), dma((3,)), dma((4,)), dma((4,)), dma(()),
        ],
        compiler_params=pltpu.CompilerParams(
            collective_id=0, has_side_effects=True, vmem_limit_bytes=48 * 1024 * 1024
        ),
        cost_estimate=pl.CostEstimate(flops=20_000_000_000, bytes_accessed=10_000_000, transcendentals=0),
    )(kspace, coil_maps, sample_mask, jnp.asarray(row_tables()), jnp.asarray(col_tables()))


def solution(mesh):
    return jax.shard_map(
        on_device,
        mesh=mesh,
        in_specs=(
            P("bin", "coil", None, None, None, None),
            P("coil", None, None, None, None),
            P("bin", None, None),
        ),
        out_specs=P("bin", None, None, None, None),
        check_vma=False,
    )
```

time: 888 us -> 135 us (0.15)
  the two profiles are of different devices: /device:TPU:2 before, /device:TPU:1 now
where the time goes in v1:
time: 135 us
  Pallas kernels  129 us (96%)
  local copies, waits for them, and re-layouts  6.06 us (4%)
    pallas_call x1, Pallas kernels, on_device(): pl.pallas_call(kernel, out_shape=jax.ShapeDtypeStruct((2, SL) + PLANE, F3...  129 us
    unnamed x9, local copies, waits for them, and re-layouts  6.06 us

profile of v1, /device:TPU:1, one launch (start us, length us, event | category | flops | bytes accessed | tf_op | source)
XLA Modules:
  0.0 135.1 jit_solution(540531126100113902)
XLA Ops:
  0.0 0.0 copy-start
  0.0 1.4 %copy-done = f32[2,4,2,96,256]{4,3,2,1,0:T(8,128)S(1)} copy-done((f32[2,4,2,96,256]{4,3,2,1,0:T(8,128)S(1)}, f32[2,4,2,96,256]{4,3,2,1,0:T(8,128)}, u32[]{:S(2)}) %copy-start) | copy-done | bytes 1572888
  1.4 0.0 copy-start.1
  1.4 0.9 copy-done.1
  2.3 0.0 copy-start.2
  2.3 1.6 %copy-done.2 = bf16[2,2,512,512]{3,2,1,0:T(8,128)(2,1)S(1)} copy-done((bf16[2,2,512,512]{3,2,1,0:T(8,128)(2,1)S(1)}, bf16[2,2,512,512]{3,2,1,0:T(8,128)(2,1)}, u32[]{:S(2)}) %copy-start.2) | copy-done | bytes 2097176
  3.9 0.0 copy-start.3
  3.9 1.0 copy-done.3
  4.9 129.1 %shard_map.55 = f32[2,4,2,96,256]{4,3,2,1,0:T(8,128)S(1)} custom-call(f32[2,2,4,2,96,256]{5,4,3,2,1,0:T(8,128)} %kspace.1, f32[2,4,2,96,256]{4,3,2,1,0:T(8,128)S(1)} %copy-done, s32[2,96,256]{2,1,0:T(8,128)S(1)} %copy-done.1, bf16[2,2,512,512]{3,2,1,0:T(8,128)(2,1)S(1)} %copy-done.2, bf16[2,2,192,192]{3,2,1,0:T(8,128)(2,1)S(1)} %copy-done.3), custom_call_target="tpu_custom_call" | custom-call | flops 20000000000 | bytes 10000000 | tf_op jit(solution)/shard_map/pallas_call | solution.py:319
  134.0 1.1 copy.7
Async XLA Ops:
  0.0 1.4 %copy-start = (f32[2,4,2,96,256]{4,3,2,1,0:T(8,128)S(1)}, f32[2,4,2,96,256]{4,3,2,1,0:T(8,128)}, u32[]{:S(2)}) copy-start(f32[2,4,2,96,256]{4,3,2,1,0:T(8,128)} %coil_maps.1) | copy-start | bytes 4718596
  1.4 0.9 copy-start.1
  2.3 1.6 %copy-start.2 = (bf16[2,2,512,512]{3,2,1,0:T(8,128)(2,1)S(1)}, bf16[2,2,512,512]{3,2,1,0:T(8,128)(2,1)}, u32[]{:S(2)}) copy-start(bf16[2,2,512,512]{3,2,1,0:T(8,128)(2,1)} %constant.4.clone.row_table) | copy-start | bytes 6291460
  3.9 1.0 copy-start.3

commit v2 on v1

v2 whole, which is shorter than its diff:
```python
import math

import jax
import jax.numpy as jnp
import numpy as np
from jax import lax
from jax.experimental import pallas as pl
from jax.experimental.pallas import tpu as pltpu
from jax.sharding import PartitionSpec as P

MESH = pl.DeviceIdType.MESH
F32 = jnp.float32
BF16 = jnp.bfloat16
NZ, NY, SL = 96, 256, 4
BIN_AXIS, COIL_AXIS = 16, 16
BINS = 32
COUNT = (BINS - 1) * SL * NZ * NY
PLANE = (2, NZ, NY)
HALF = NZ // 2


def dft_tables(length):
    index = np.arange(length)
    angle = (index[:, None] * index[None, :] % length) * (2.0 * math.pi / length)
    factor = 1.0 / math.sqrt(length)
    return np.cos(angle) * factor, np.sin(angle) * factor


def halves(table):
    high = table.astype(np.float32).astype(jnp.bfloat16)
    low = (table - high.astype(np.float64)).astype(np.float32).astype(jnp.bfloat16)
    return np.stack([high, low])


def row_tables():
    cos, sin = dft_tables(NY)
    forward = np.block([[cos, -sin], [sin, cos]])
    return np.stack([halves(forward), halves(forward.T)])


def col_tables():
    cos, sin = dft_tables(NZ)
    forward = np.block([[cos, sin], [-sin, cos]])
    return np.stack([halves(forward), halves(forward.T)])


def split(values):
    high = values.astype(BF16)
    return high, (values - high.astype(F32)).astype(BF16)


def dot(left, right):
    return jnp.dot(left, right, preferred_element_type=F32)


def rows(high, low, table, which):
    return dot(high, table[which, 0]) + dot(low, table[which, 0]) + dot(high, table[which, 1])


def cols(values, table, which):
    high, low = split(values)
    return dot(table[which, 0], high) + dot(table[which, 0], low) + dot(table[which, 1], high)


def fold(values):
    part = jnp.sum(values.reshape(values.shape[0] // 8, 8, NY), axis=0)
    return part[:, :128] + part[:, 128:]


def total(values):
    return jnp.sum(values, keepdims=True)


def kernel(
    kspace, coil_maps, mask, row_table, col_table, out,
    samples, own_maps, ticks, row, col, maps, weight, high, low, mid,
    part, from_sib, to_y, from_y, to_z, from_z,
    rhs, quad, resid, image, near_rhs, near_resid, message, sums,
    load_sem, sample_sem, slot_sem,
    map_send, map_recv, turn_send, turn_recv, map_sib_send, map_sib_recv,
    sib_send, sib_recv, y_send, y_recv, z_send, z_recv,
    near_send, near_recv, sum_send, sum_recv,
    out_send, out_recv, out_sib_send, out_sib_recv, out_local,
):
    b = lax.axis_index("bin")
    j = lax.axis_index("coil")
    y, z, c = j // 4, (j // 2) % 2, j % 2
    x = lax.rem(b, 4)
    ring = z * 4 + b // 4

    def at_y(step):
        return (b, lax.rem(y + step, 4) * 4 + z * 2 + c)

    def at_xz(step_x, step_z, core):
        place = lax.rem(ring + step_z + 8, 8)
        return (
            lax.rem(place, 4) * 4 + lax.rem(x + step_x + 4, 4),
            y * 4 + place // 4 * 2 + core,
        )

    sibling = (b, j + 1 - 2 * c)
    opposite = (b, j + 2 - 4 * z)
    wraps = jnp.where(c == 1, jnp.where(x == 3, 1, 0), jnp.where(x == 0, -1, 0))
    across = at_xz(2 * c - 1, wraps, 1 - c)
    coil_peers = [(b, lax.rem(j + step, COIL_AXIS)) for step in range(1, COIL_AXIS)]
    image_peers = [
        (b, lax.rem(y + step // 2, 4) * 4 + z * 2 + lax.rem(c + step, 2)) for step in range(1, 8)
    ]
    steps = [(dx, dz) for dz in (0, 1, 2, -1) for dx in range(4)][1:]
    bin_peers = [at_xz(dx, dz, c) for dx, dz in steps]

    def remote(source, target, send_sem, recv_sem, device):
        return pltpu.make_async_remote_copy(
            src_ref=source, dst_ref=target, send_sem=send_sem, recv_sem=recv_sem,
            device_id=device, device_id_type=MESH,
        )

    def send(*args):
        copy = remote(*args)
        copy.start()
        return copy

    def load(source, target, sem):
        copy = pltpu.make_async_copy(source, target, sem)
        copy.start()
        return copy

    def sample_copy(k):
        return pltpu.make_async_copy(
            kspace.at[:, :, lax.rem(y + 3 - k, 4)], samples.at[k], sample_sem.at[k]
        )

    barrier = pltpu.get_barrier_semaphore()
    greeted = coil_peers + [at_xz(-dx, -dz, c) for dx, dz in steps] + [across]
    for device in greeted:
        pl.semaphore_signal(barrier, inc=1, device_id=device, device_id_type=MESH)
    loads = [load(mask, ticks, load_sem.at[0]), load(row_table.at[1], row.at[1], load_sem.at[1])]
    sample_copy(0).start()
    loads += [load(col_table, col, load_sem.at[2]), load(coil_maps, own_maps, load_sem.at[3])]
    for k in (1, 2, 3):
        sample_copy(k).start()
    late_load = load(row_table.at[0], row.at[0], load_sem.at[4])
    slot_copy = load(coil_maps.at[:, y], maps.at[0, c], slot_sem)
    pl.semaphore_wait(barrier, len(greeted))

    quarter = pl.ds(pl.multiple_of(x * (NZ // 4), 8), NZ // 4)
    map_copies = [
        send(coil_maps.at[:, lax.rem(y + step, 4), :, quarter], maps.at[4 - step, c, :, :, quarter],
             map_send.at[step - 1], map_recv.at[4 - step - 1], at_y(step))
        for step in (1, 2, 3)
    ]
    sib_maps = [send(coil_maps.at[:, y], maps.at[0, c], map_sib_send.at[0], map_sib_recv.at[0], sibling)]
    loads[0].wait()
    weight[0] = ticks[0].astype(F32)
    weight[1] = ticks[1].astype(F32)
    for copy in loads[1:]:
        copy.wait()

    def half(h):
        return pl.ds(pl.multiple_of(h * HALF, 16), HALF)

    def sib_copy(k):
        return remote(part.at[k, 1 - c], from_sib.at[k], sib_send.at[k], sib_recv.at[k], sibling)

    def y_copy(k, h):
        return remote(
            to_y.at[k, :, half(h)], from_y.at[k, :, half(h)], y_send.at[k, h], y_recv.at[k, h], at_y(3 - k)
        )

    def z_copy(n, h):
        return remote(
            to_z.at[n, :, half(h)], from_z.at[n, :, half(h)], z_send.at[n, h], z_recv.at[n, h], opposite
        )

    def adjoint(k, carry):
        s = lax.rem(y + 3 - k, 4)
        sample_copy(k).wait()
        for t in range(4):
            w = weight[t // 2]
            values = jnp.concatenate(
                [samples[k, t // 2, t % 2, 0] * w, samples[k, t // 2, t % 2, 1] * w], axis=1
            )
            high[0, t * NZ:(t + 1) * NZ], low[0, t * NZ:(t + 1) * NZ] = split(values)
        used = pl.ds(0, 4 * NZ)
        mid[0, used] = rows(high[0, used], low[0, used], row, 1)
        for bin_ in range(2):
            sum_re, sum_im = 0.0, 0.0
            for coil in range(2):
                at = pl.ds((bin_ * 2 + coil) * NZ, NZ)
                wave = cols(jnp.concatenate([mid[0, at, :NY], mid[0, at, NY:]], axis=0), col, 1)
                sens_re, sens_im = own_maps[coil, s, 0], own_maps[coil, s, 1]
                sum_re += sens_re * wave[:NZ] + sens_im * wave[NZ:]
                sum_im += sens_re * wave[NZ:] - sens_im * wave[:NZ]
            part[k, bin_, 0] = sum_re
            part[k, bin_, 1] = sum_im
        sib_copy(k).start()

        @pl.when(k > 0)
        def _():
            sib_copy(k - 1).wait_recv()
            to_y[k - 1] = part[k - 1, c] + from_sib[k - 1]
            y_copy(k - 1, 0).start()

        return carry

    lax.fori_loop(0, 4, adjoint, 0)
    for k in range(3):
        y_copy(k, 1).start()
    for copy in map_copies:
        copy.wait_recv()
    slots = maps.at[pl.ds(1, 3), c, :, :, quarter]
    turns = [
        send(slots, slots, turn_send.at[step - 1], turn_recv.at[step - 1], at_xz(step, 0, c))
        for step in (1, 2, 3)
    ]
    sib_copy(3).wait_recv()
    for h in range(2):
        at = half(h)
        own = part[3, c, :, at] + from_sib[3, :, at]
        for k in range(3):
            y_copy(k, h).wait_recv()
            own = own + from_y[k, :, at]
        to_z[0, :, at] = own
        z_copy(0, h).start()
    for copy in turns:
        copy.wait_recv()
    slots = maps.at[pl.ds(1, 3), c]
    sib_maps.append(send(slots, slots, map_sib_send.at[1], map_sib_recv.at[1], sibling))
    slot_copy.wait()
    late_load.wait()

    def spread(field, h):
        at = half(h)
        field_re, field_im = field[0, at], field[1, at]

        def one(n, carry):
            for t in range(4):
                sens_re, sens_im = maps[n, t // 2, t % 2, 0, at], maps[n, t // 2, t % 2, 1, at]
                values = jnp.concatenate(
                    [sens_re * field_re - sens_im * field_im, sens_re * field_im + sens_im * field_re], axis=1
                )
                to = pl.ds(pl.multiple_of((n * 4 + t) * HALF, 16), HALF)
                high[h, to], low[h, to] = split(values)
            return carry

        lax.fori_loop(0, 4, one, 0)
        mid[h] = rows(high[h], low[h], row, 0)

    def masked(n):
        at = pl.ds(pl.multiple_of(n * HALF, 16), HALF)
        values = cols(
            jnp.concatenate([mid[0, at, :NY], mid[1, at, :NY], mid[0, at, NY:], mid[1, at, NY:]], axis=0), col, 0
        )
        w = weight[c]
        return values * jnp.concatenate([w, w], axis=0), at

    def normal(n, energy):
        for t in range(4):
            values, at = masked(n * 4 + t)
            energy = energy + fold(values * values)
            wave = cols(values, col, 1)
            for h in range(2):
                lines = jnp.concatenate(
                    [wave[h * HALF:(h + 1) * HALF], wave[NZ + h * HALF:NZ + (h + 1) * HALF]], axis=1
                )
                high[h, at], low[h, at] = split(lines)
        return energy

    def gather(h, carry):
        mid[h] = rows(high[h], low[h], row, 1)
        at = half(h)

        def one(n, sums_):
            sum_re, sum_im = sums_
            for t in range(4):
                lines = pl.ds(pl.multiple_of((n * 4 + t) * HALF, 16), HALF)
                sens_re, sens_im = maps[n, t // 2, t % 2, 0, at], maps[n, t // 2, t % 2, 1, at]
                sum_re += sens_re * mid[h, lines, :NY] + sens_im * mid[h, lines, NY:]
                sum_im += sens_re * mid[h, lines, NY:] - sens_im * mid[h, lines, :NY]
            return sum_re, sum_im

        none = jnp.zeros((HALF, NY), F32)
        to_z[1, 0, at], to_z[1, 1, at] = lax.fori_loop(0, 4, one, (none, none))
        z_copy(1, h).start()
        return carry

    def forward(n, energy):
        for t in range(4):
            values, _ = masked(n * 4 + t)
            energy = energy + fold(values * values)
        return energy

    def inner(left, right):
        return fold(left[0] * right[0] + left[1] * right[1])

    lane = lax.broadcasted_iota(jnp.int32, (1, 128), 1)

    def share(which, stage, peers, me):
        copies = [
            send(message.at[which, stage], sums.at[which, stage, me],
                 sum_send.at[which, stage, n], sum_recv.at[which, stage, n], peer)
            for n, peer in enumerate(peers)
        ]
        sums[which, stage, me] = message[which, stage]
        return copies

    def collect(which, stage, copies):
        for copy in copies:
            copy.wait()
        return jnp.sum(sums[which, stage, :len(copies) + 1], axis=0)

    def reduce_start(which, parts):
        line = jnp.zeros((1, 128), F32)
        for n, value in enumerate(parts):
            line = jnp.where(lane == n, total(value), line)
        message[which, 0] = line
        peers, me = (image_peers, y * 2 + c) if which == 2 else (coil_peers, j)
        return share(which, 0, peers, me)

    def reduce_end(which, copies, count):
        message[which, 1] = collect(which, 0, copies)
        line = collect(which, 1, share(which, 1, bin_peers, b))
        return [line[:, n:n + 1] for n in range(count)]

    zero = jnp.zeros((8, 128), F32)
    for copy in sib_maps:
        copy.wait_recv()
    for h in range(2):
        at = half(h)
        z_copy(0, h).wait_recv()
        rhs[:, at] = to_z[0, :, at] + from_z[0, :, at]
        spread(rhs, h)
    near = [
        send(rhs, near_rhs.at[0], near_send.at[0], near_recv.at[0], sibling),
        send(rhs, near_rhs.at[1], near_send.at[1], near_recv.at[1], across),
    ]
    energy = lax.fori_loop(0, 4, normal, zero)
    copies = reduce_start(0, [0.5 * inner(rhs, rhs), energy])
    lax.fori_loop(0, 2, gather, 0)
    norm_0, energy_0 = reduce_end(0, copies, 2)
    curve_0 = energy_0 + 0.1 * norm_0
    alpha_0 = norm_0 / curve_0
    for h in range(2):
        at = half(h)
        z_copy(1, h).wait_recv()
        quad[:, at] = to_z[1, :, at] + from_z[1, :, at] + 0.1 * rhs[:, at]
        resid[:, at] = rhs[:, at] - alpha_0 * quad[:, at]
        spread(resid, h)
    near += [
        send(resid, near_resid.at[0], near_send.at[2], near_recv.at[2], sibling),
        send(resid, near_resid.at[1], near_send.at[3], near_recv.at[3], across),
    ]
    energy = lax.fori_loop(0, 4, forward, zero)
    copies = reduce_start(1, [0.5 * inner(resid, resid), 0.5 * inner(resid, quad), energy])
    norm_1, cross, energy_1 = reduce_end(1, copies, 3)
    beta = norm_1 / norm_0
    curve_1 = energy_1 + 0.1 * norm_1 + 2.0 * beta * cross + beta * beta * curve_0
    alpha_1 = norm_1 / curve_1
    on_rhs = alpha_0 + alpha_1 * beta
    for copy in near:
        copy.wait()
    here = on_rhs * rhs[...] + alpha_1 * resid[...]
    after = on_rhs * near_rhs[c] + alpha_1 * near_resid[c]
    me = 2 * b + c
    diff = jnp.where(me < BINS - 1, after - here, 0.0)
    size = jnp.sqrt(diff[0] * diff[0] + diff[1] * diff[1])
    copies = reduce_start(2, [fold(size)])
    before = on_rhs * near_rhs[1 - c] + alpha_1 * near_resid[1 - c]
    prior = jnp.where(me > 0, here - before, 0.0)
    prior_size = jnp.sqrt(prior[0] * prior[0] + prior[1] * prior[1])
    (size_sum,) = reduce_end(2, copies, 1)
    lam = size_sum / COUNT + 1e-06
    scale = lam / jnp.maximum(size, lam)
    prior_scale = lam / jnp.maximum(prior_size, lam)
    image[...] = here + 0.25 * (diff * scale[None] - prior * prior_scale[None])

    own_out = pltpu.make_async_copy(image, out.at[c, y], out_local)
    own_out.start()
    copies = [
        send(image, out.at[c, y], out_send.at[step - 1], out_recv.at[4 - step - 1], at_y(step))
        for step in (1, 2, 3)
    ]
    sib_copies = [send(image, out.at[c, y], out_sib_send.at[0], out_sib_recv.at[0], sibling)]
    for slot in (1, 3, 2):
        copies[3 - slot].wait_recv()
        there = out.at[c, lax.rem(y + slot, 4)]
        sib_copies.append(send(there, there, out_sib_send.at[slot], out_sib_recv.at[slot], sibling))
    own_out.wait()
    for k in range(4):
        sib_copy(k).wait_send()
    for k in range(3):
        for h in range(2):
            y_copy(k, h).wait_send()
        map_copies[k].wait_send()
        turns[k].wait_send()
        copies[k].wait_send()
    for n in range(2):
        for h in range(2):
            z_copy(n, h).wait_send()
    for copy in sib_maps:
        copy.wait_send()
    for copy in sib_copies:
        copy.wait()


def on_device(kspace, coil_maps, sample_mask):
    dma = pltpu.SemaphoreType.DMA
    whole = pl.BlockSpec(memory_space=pl.ANY)
    return pl.pallas_call(
        kernel,
        out_shape=jax.ShapeDtypeStruct((2, SL) + PLANE, F32),
        in_specs=[whole] * 5,
        out_specs=whole,
        scratch_shapes=[
            pltpu.VMEM((4, 2, 2) + PLANE, F32),
            pltpu.VMEM((2, SL) + PLANE, F32),
            pltpu.VMEM(PLANE, jnp.int32),
            pltpu.VMEM((2, 2, 2 * NY, 2 * NY), BF16),
            pltpu.VMEM((2, 2, 2 * NZ, 2 * NZ), BF16),
            pltpu.VMEM((4, 2, 2) + PLANE, F32),
            pltpu.VMEM(PLANE, F32),
            pltpu.VMEM((2, 16 * HALF, 2 * NY), BF16),
            pltpu.VMEM((2, 16 * HALF, 2 * NY), BF16),
            pltpu.VMEM((2, 16 * HALF, 2 * NY), F32),
            pltpu.VMEM((4, 2) + PLANE, F32),
            pltpu.VMEM((4,) + PLANE, F32),
            pltpu.VMEM((3,) + PLANE, F32),
            pltpu.VMEM((3,) + PLANE, F32),
            pltpu.VMEM((2,) + PLANE, F32),
            pltpu.VMEM((2,) + PLANE, F32),
            pltpu.VMEM(PLANE, F32),
            pltpu.VMEM(PLANE, F32),
            pltpu.VMEM(PLANE, F32),
            pltpu.VMEM(PLANE, F32),
            pltpu.VMEM((2,) + PLANE, F32),
            pltpu.VMEM((2,) + PLANE, F32),
            pltpu.VMEM((3, 2, 1, 128), F32),
            pltpu.VMEM((3, 2, 16, 1, 128), F32),
            dma((5,)), dma((4,)), dma(()),
            dma((3,)), dma((3,)), dma((3,)), dma((3,)), dma((2,)), dma((2,)),
            dma((4,)), dma((4,)), dma((3, 2)), dma((3, 2)), dma((2, 2)), dma((2, 2)),
            dma((4,)), dma((4,)), dma((3, 2, 15)), dma((3, 2, 15)),
            dma((3,)), dma((3,)), dma((4,)), dma((4,)), dma(()),
        ],
        compiler_params=pltpu.CompilerParams(
            collective_id=0, has_side_effects=True, vmem_limit_bytes=60 * 1024 * 1024
        ),
        cost_estimate=pl.CostEstimate(flops=20_000_000_000, bytes_accessed=10_000_000, transcendentals=0),
    )(kspace, coil_maps, sample_mask, jnp.asarray(row_tables()), jnp.asarray(col_tables()))


def solution(mesh):
    return jax.shard_map(
        on_device,
        mesh=mesh,
        in_specs=(
            P("bin", "coil", None, None, None, None),
            P("coil", None, None, None, None),
            P("bin", None, None),
        ),
        out_specs=P("bin", None, None, None, None),
        check_vma=False,
    )
```

time: 135 us -> 98.6 us (0.73)
  Pallas kernels: 129 us -> 95.8 us
  local copies, waits for them, and re-layouts: 6.06 us -> 2.69 us
    pallas_call x1, Pallas kernels: 129 us -> 95.8 us  [on_device(): pl.pallas_call(kernel, out_shape=jax.ShapeDtypeStruct((2, SL) + PLANE, F3...]
    unnamed x9 -> x1, local copies, waits for them, and re-layouts: 6.06 us -> 2.69 us
where the time goes in v2:
time: 98.6 us; the launch traced here: 98.5 us
  Pallas kernels  95.8 us (97%)
  local copies, waits for them, and re-layouts  2.69 us (3%)
    pallas_call x1, Pallas kernels, on_device(): pl.pallas_call(kernel, out_shape=jax.ShapeDtypeStruct((2, SL) + PLANE, F3...  95.8 us
    unnamed x1, local copies, waits for them, and re-layouts  2.69 us

profile of v2, /device:TPU:1, one launch (start us, length us, event | category | flops | bytes accessed | tf_op | source)
XLA Modules:
  0.0 98.5 jit_solution(16267532739378826130)
XLA Ops:
  0.0 95.8 %shard_map.55 = f32[2,4,2,96,256]{4,3,2,1,0:T(8,128)} custom-call(f32[2,2,4,2,96,256]{5,4,3,2,1,0:T(8,128)} %kspace.1, f32[2,4,2,96,256]{4,3,2,1,0:T(8,128)} %coil_maps.1, s32[2,96,256]{2,1,0:T(8,128)} %mask.1, bf16[2,2,512,512]{3,2,1,0:T(8,128)(2,1)} %constant.4.clone.row_table, bf16[2,2,192,192]{3,2,1,0:T(8,128)(2,1)} %constant.5.clone.col_table), custom_call_target="tpu_custom_call" | custom-call | flops 20000000000 | bytes 10000000 | tf_op jit(solution)/shard_map/pallas_call | solution.py:409
  95.8 2.7 %copy.7 = f32[2,4,2,96,256]{4,3,2,1,0:T(8,128)} copy(f32[2,4,2,96,256]{4,3,2,1,0:T(8,128)} %shard_map.55) | data formatting | bytes 3145728

commit v3 on v2

--- a/solution.py
+++ b/solution.py
@@ -75,12 +75,12 @@
     kspace, coil_maps, mask, row_table, col_table, out,
     samples, own_maps, ticks, row, col, maps, weight, high, low, mid,
     part, from_sib, to_y, from_y, to_z, from_z,
-    rhs, quad, resid, image, near_rhs, near_resid, message, sums,
+    fields, quad, gaps, sizes, result, message, sums,
     load_sem, sample_sem, slot_sem,
     map_send, map_recv, turn_send, turn_recv, map_sib_send, map_sib_recv,
     sib_send, sib_recv, y_send, y_recv, z_send, z_recv,
-    near_send, near_recv, sum_send, sum_recv,
-    out_send, out_recv, out_sib_send, out_sib_recv, out_local,
+    near_send, near_recv, along_send, along_recv, pass_send, pass_recv, far_send, far_recv,
+    sum_send, sum_recv, out_sem,
 ):
     b = lax.axis_index("bin")
     j = lax.axis_index("coil")
@@ -98,6 +98,8 @@
             y * 4 + place // 4 * 2 + core,
         )
 
+    rhs = fields.at[0, 1 + c, y]
+    resid = fields.at[1, 1 + c, y]
     sibling = (b, j + 1 - 2 * c)
     opposite = (b, j + 2 - 4 * z)
     wraps = jnp.where(c == 1, jnp.where(x == 3, 1, 0), jnp.where(x == 0, -1, 0))
@@ -317,10 +319,52 @@
         peers, me = (image_peers, y * 2 + c) if which == 2 else (coil_peers, j)
         return share(which, 0, peers, me)
 
-    def reduce_end(which, copies, count):
+    def reduce_end(which, copies, count, meanwhile):
         message[which, 1] = collect(which, 0, copies)
-        line = collect(which, 1, share(which, 1, bin_peers, b))
+        copies = share(which, 1, bin_peers, b)
+        meanwhile()
+        line = collect(which, 1, copies)
         return [line[:, n:n + 1] for n in range(count)]
+
+    near, along, onward, far = [], [], [], []
+
+    def publish(n):
+        mine = fields.at[n, 1 + c, y]
+        near.append([
+            send(mine, mine, near_send.at[n, 0], near_recv.at[n, 0], sibling),
+            send(mine, fields.at[n, 3 - 3 * c, y], near_send.at[n, 1], near_recv.at[n, 1], across),
+        ])
+        along.append([
+            send(mine, mine, along_send.at[n, step - 1], along_recv.at[n, 4 - step - 1], at_y(step))
+            for step in (1, 2, 3)
+        ])
+
+    def pass_on(n):
+        onward.append([])
+        for slot in (1, 3, 2):
+            along[n][3 - slot].wait_recv()
+            line = lax.rem(y + slot, 4)
+            plane = fields.at[n, 1 + c, line]
+            onward[n] += [
+                send(plane, plane, pass_send.at[n, 0, slot - 1], pass_recv.at[n, 0, slot - 1], sibling),
+                send(plane, fields.at[n, 3 - 3 * c, line],
+                     pass_send.at[n, 1, slot - 1], pass_recv.at[n, 1, slot - 1], across),
+            ]
+
+    def greet(n):
+        for copy in near[n]:
+            copy.wait_recv()
+
+    def hand_over(n):
+        for copy in onward[n][1::2]:
+            copy.wait_recv()
+        planes = fields.at[n, 3 * c]
+        far.append(send(planes, planes, far_send.at[n], far_recv.at[n], sibling))
+
+    def settle(n):
+        for copy in onward[n][::2]:
+            copy.wait_recv()
+        far[n].wait_recv()
 
     zero = jnp.zeros((8, 128), F32)
     for copy in sib_maps:
@@ -330,14 +374,11 @@
         z_copy(0, h).wait_recv()
         rhs[:, at] = to_z[0, :, at] + from_z[0, :, at]
         spread(rhs, h)
-    near = [
-        send(rhs, near_rhs.at[0], near_send.at[0], near_recv.at[0], sibling),
-        send(rhs, near_rhs.at[1], near_send.at[1], near_recv.at[1], across),
-    ]
+    publish(0)
     energy = lax.fori_loop(0, 4, normal, zero)
     copies = reduce_start(0, [0.5 * inner(rhs, rhs), energy])
     lax.fori_loop(0, 2, gather, 0)
-    norm_0, energy_0 = reduce_end(0, copies, 2)
+    norm_0, energy_0 = reduce_end(0, copies, 2, lambda: pass_on(0))
     curve_0 = energy_0 + 0.1 * norm_0
     alpha_0 = norm_0 / curve_0
     for h in range(2):
@@ -346,46 +387,61 @@
         quad[:, at] = to_z[1, :, at] + from_z[1, :, at] + 0.1 * rhs[:, at]
         resid[:, at] = rhs[:, at] - alpha_0 * quad[:, at]
         spread(resid, h)
-    near += [
-        send(resid, near_resid.at[0], near_send.at[2], near_recv.at[2], sibling),
-        send(resid, near_resid.at[1], near_send.at[3], near_recv.at[3], across),
-    ]
+    publish(1)
+    greet(0)
+    hand_over(0)
     energy = lax.fori_loop(0, 4, forward, zero)
     copies = reduce_start(1, [0.5 * inner(resid, resid), 0.5 * inner(resid, quad), energy])
-    norm_1, cross, energy_1 = reduce_end(1, copies, 3)
+    norm_1, cross, energy_1 = reduce_end(1, copies, 3, lambda: pass_on(1))
     beta = norm_1 / norm_0
     curve_1 = energy_1 + 0.1 * norm_1 + 2.0 * beta * cross + beta * beta * curve_0
     alpha_1 = norm_1 / curve_1
     on_rhs = alpha_0 + alpha_1 * beta
-    for copy in near:
-        copy.wait()
-    here = on_rhs * rhs[...] + alpha_1 * resid[...]
-    after = on_rhs * near_rhs[c] + alpha_1 * near_resid[c]
-    me = 2 * b + c
-    diff = jnp.where(me < BINS - 1, after - here, 0.0)
-    size = jnp.sqrt(diff[0] * diff[0] + diff[1] * diff[1])
-    copies = reduce_start(2, [fold(size)])
-    before = on_rhs * near_rhs[1 - c] + alpha_1 * near_resid[1 - c]
-    prior = jnp.where(me > 0, here - before, 0.0)
-    prior_size = jnp.sqrt(prior[0] * prior[0] + prior[1] * prior[1])
-    (size_sum,) = reduce_end(2, copies, 1)
+    greet(1)
+
+    def iterate(place, line):
+        return on_rhs * fields[0, place, line] + alpha_1 * fields[1, place, line]
+
+    def length(gap):
+        return jnp.sqrt(gap[0] * gap[0] + gap[1] * gap[1])
+
+    gap = jnp.where(2 * b + c < BINS - 1, iterate(2 + c, y) - iterate(1 + c, y), 0.0)
+    copies = reduce_start(2, [fold(length(gap))])
+
+    def differences(line, carry):
+        values = [iterate(place, line) for place in range(4)]
+        result[line, 0] = values[1]
+        result[line, 1] = values[2]
+        for n, keep in enumerate((b > 0, None, b < BIN_AXIS - 1)):
+            gap = values[n + 1] - values[n]
+            if keep is not None:
+                gap = jnp.where(keep, gap, 0.0)
+            gaps[line, n] = gap
+            sizes[line, n] = length(gap)
+        return carry
+
+    def prepare():
+        hand_over(1)
+        settle(0)
+        settle(1)
+        lax.fori_loop(0, SL, differences, 0)
+
+    (size_sum,) = reduce_end(2, copies, 1, prepare)
     lam = size_sum / COUNT + 1e-06
-    scale = lam / jnp.maximum(size, lam)
-    prior_scale = lam / jnp.maximum(prior_size, lam)
-    image[...] = here + 0.25 * (diff * scale[None] - prior * prior_scale[None])
-
-    own_out = pltpu.make_async_copy(image, out.at[c, y], out_local)
-    own_out.start()
-    copies = [
-        send(image, out.at[c, y], out_send.at[step - 1], out_recv.at[4 - step - 1], at_y(step))
-        for step in (1, 2, 3)
-    ]
-    sib_copies = [send(image, out.at[c, y], out_sib_send.at[0], out_sib_recv.at[0], sibling)]
-    for slot in (1, 3, 2):
-        copies[3 - slot].wait_recv()
-        there = out.at[c, lax.rem(y + slot, 4)]
-        sib_copies.append(send(there, there, out_sib_send.at[slot], out_sib_recv.at[slot], sibling))
-    own_out.wait()
+
+    def out_copy(line):
+        return pltpu.make_async_copy(result.at[line], out.at[:, line], out_sem.at[line])
+
+    def finish(line, carry):
+        dual = [
+            gaps[line, n] * (lam / jnp.maximum(sizes[line, n], lam))[None] for n in range(3)
+        ]
+        for n in range(2):
+            result[line, n] = result[line, n] + 0.25 * (dual[n + 1] - dual[n])
+        out_copy(line).start()
+        return carry
+
+    lax.fori_loop(0, SL, finish, 0)
     for k in range(4):
         sib_copy(k).wait_send()
     for k in range(3):
@@ -393,14 +449,15 @@
             y_copy(k, h).wait_send()
         map_copies[k].wait_send()
         turns[k].wait_send()
-        copies[k].wait_send()
     for n in range(2):
         for h in range(2):
             z_copy(n, h).wait_send()
+        for copy in near[n] + along[n] + onward[n] + [far[n]]:
+            copy.wait_send()
     for copy in sib_maps:
         copy.wait_send()
-    for copy in sib_copies:
-        copy.wait()
+    for line in range(SL):
+        out_copy(line).wait()
 
 
 def on_device(kspace, coil_maps, sample_mask):
@@ -428,19 +485,19 @@
             pltpu.VMEM((3,) + PLANE, F32),
             pltpu.VMEM((2,) + PLANE, F32),
             pltpu.VMEM((2,) + PLANE, F32),
+            pltpu.VMEM((2, 4, SL) + PLANE, F32),
             pltpu.VMEM(PLANE, F32),
-            pltpu.VMEM(PLANE, F32),
-            pltpu.VMEM(PLANE, F32),
-            pltpu.VMEM(PLANE, F32),
-            pltpu.VMEM((2,) + PLANE, F32),
-            pltpu.VMEM((2,) + PLANE, F32),
+            pltpu.VMEM((SL, 3) + PLANE, F32),
+            pltpu.VMEM((SL, 3, NZ, NY), F32),
+            pltpu.VMEM((SL, 2) + PLANE, F32),
             pltpu.VMEM((3, 2, 1, 128), F32),
             pltpu.VMEM((3, 2, 16, 1, 128), F32),
             dma((5,)), dma((4,)), dma(()),
             dma((3,)), dma((3,)), dma((3,)), dma((3,)), dma((2,)), dma((2,)),
             dma((4,)), dma((4,)), dma((3, 2)), dma((3, 2)), dma((2, 2)), dma((2, 2)),
-            dma((4,)), dma((4,)), dma((3, 2, 15)), dma((3, 2, 15)),
-            dma((3,)), dma((3,)), dma((4,)), dma((4,)), dma(()),
+            dma((2, 2)), dma((2, 2)), dma((2, 3)), dma((2, 3)),
+            dma((2, 2, 3)), dma((2, 2, 3)), dma((2,)), dma((2,)),
+            dma((3, 2, 15)), dma((3, 2, 15)), dma((SL,)),
         ],
         compiler_params=pltpu.CompilerParams(
             collective_id=0, has_side_effects=True, vmem_limit_bytes=60 * 1024 * 1024

time: 98.6 us -> 91.1 us (0.924)
  Pallas kernels: 95.8 us -> 88.3 us
    pallas_call x1, Pallas kernels: 95.8 us -> 88.3 us  [on_device(): pl.pallas_call(kernel, out_shape=jax.ShapeDtypeStruct((2, SL) + PLANE, F3...]
where the time goes in v3:
time: 91.1 us; the launch traced here: 91 us
  Pallas kernels  88.3 us (97%)
  local copies, waits for them, and re-layouts  2.69 us (3%)
    pallas_call x1, Pallas kernels, on_device(): pl.pallas_call(kernel, out_shape=jax.ShapeDtypeStruct((2, SL) + PLANE, F3...  88.3 us
    unnamed x1, local copies, waits for them, and re-layouts  2.69 us

profile of v3, /device:TPU:1, one launch (start us, length us, event | category | flops | bytes accessed | tf_op | source)
XLA Modules:
  0.0 91.0 jit_solution(164848317417384310)
XLA Ops:
  0.0 88.3 %shard_map.55 = f32[2,4,2,96,256]{4,3,2,1,0:T(8,128)} custom-call(f32[2,2,4,2,96,256]{5,4,3,2,1,0:T(8,128)} %kspace.1, f32[2,4,2,96,256]{4,3,2,1,0:T(8,128)} %coil_maps.1, s32[2,96,256]{2,1,0:T(8,128)} %mask.1, bf16[2,2,512,512]{3,2,1,0:T(8,128)(2,1)} %constant.4.clone.row_table, bf16[2,2,192,192]{3,2,1,0:T(8,128)(2,1)} %constant.5.clone.col_table), custom_call_target="tpu_custom_call" | custom-call | flops 20000000000 | bytes 10000000 | tf_op jit(solution)/shard_map/pallas_call | solution.py:466
  88.4 2.7 %copy.7 = f32[2,4,2,96,256]{4,3,2,1,0:T(8,128)} copy(f32[2,4,2,96,256]{4,3,2,1,0:T(8,128)} %shard_map.55) | data formatting | bytes 3145728

commit v4 on v3

--- a/solution.py
+++ b/solution.py
@@ -104,12 +104,13 @@
     opposite = (b, j + 2 - 4 * z)
     wraps = jnp.where(c == 1, jnp.where(x == 3, 1, 0), jnp.where(x == 0, -1, 0))
     across = at_xz(2 * c - 1, wraps, 1 - c)
-    coil_peers = [(b, lax.rem(j + step, COIL_AXIS)) for step in range(1, COIL_AXIS)]
-    image_peers = [
-        (b, lax.rem(y + step // 2, 4) * 4 + z * 2 + lax.rem(c + step, 2)) for step in range(1, 8)
+    column_peers = [at_xz(0, step // 2, lax.rem(c + step, 2)) for step in range(1, 16)]
+    near_peers = [
+        at_xz(0, dz, core) for dz in (0, 1, 2, -1) for core in (c, 1 - c)
+    ][1:]
+    plane_peers = [
+        (b - x + lax.rem(x + step % 4, 4), lax.rem(y + step // 4, 4) * 4 + z * 2 + c) for step in range(1, 16)
     ]
-    steps = [(dx, dz) for dz in (0, 1, 2, -1) for dx in range(4)][1:]
-    bin_peers = [at_xz(dx, dz, c) for dx, dz in steps]
 
     def remote(source, target, send_sem, recv_sem, device):
         return pltpu.make_async_remote_copy(
@@ -122,6 +123,12 @@
         copy.start()
         return copy
 
+    def arrived(ref, sem):
+        remote(ref, ref, sem, sem, sibling).wait_recv()
+
+    def departed(ref, sem):
+        remote(ref, ref, sem, sem, sibling).wait_send()
+
     def load(source, target, sem):
         copy = pltpu.make_async_copy(source, target, sem)
         copy.start()
@@ -133,7 +140,7 @@
         )
 
     barrier = pltpu.get_barrier_semaphore()
-    greeted = coil_peers + [at_xz(-dx, -dz, c) for dx, dz in steps] + [across]
+    greeted = column_peers + plane_peers + [across]
     for device in greeted:
         pl.semaphore_signal(barrier, inc=1, device_id=device, device_id_type=MESH)
     loads = [load(mask, ticks, load_sem.at[0]), load(row_table.at[1], row.at[1], load_sem.at[1])]
@@ -143,15 +150,6 @@
         sample_copy(k).start()
     late_load = load(row_table.at[0], row.at[0], load_sem.at[4])
     slot_copy = load(coil_maps.at[:, y], maps.at[0, c], slot_sem)
-    pl.semaphore_wait(barrier, len(greeted))
-
-    quarter = pl.ds(pl.multiple_of(x * (NZ // 4), 8), NZ // 4)
-    map_copies = [
-        send(coil_maps.at[:, lax.rem(y + step, 4), :, quarter], maps.at[4 - step, c, :, :, quarter],
-             map_send.at[step - 1], map_recv.at[4 - step - 1], at_y(step))
-        for step in (1, 2, 3)
-    ]
-    sib_maps = [send(coil_maps.at[:, y], maps.at[0, c], map_sib_send.at[0], map_sib_recv.at[0], sibling)]
     loads[0].wait()
     weight[0] = ticks[0].astype(F32)
     weight[1] = ticks[1].astype(F32)
@@ -166,7 +164,7 @@
 
     def y_copy(k, h):
         return remote(
-            to_y.at[k, :, half(h)], from_y.at[k, :, half(h)], y_send.at[k, h], y_recv.at[k, h], at_y(3 - k)
+            to_y.at[k, :, half(h)], from_y.at[k, :, half(h)], y_send, y_recv.at[h], at_y(3 - k)
         )
 
     def z_copy(n, h):
@@ -195,39 +193,38 @@
                 sum_im += sens_re * wave[NZ:] - sens_im * wave[:NZ]
             part[k, bin_, 0] = sum_re
             part[k, bin_, 1] = sum_im
+        return carry
+
+    lax.fori_loop(0, 4, adjoint, 0)
+    pl.semaphore_wait(barrier, len(greeted))
+    for k in range(4):
         sib_copy(k).start()
-
-        @pl.when(k > 0)
-        def _():
-            sib_copy(k - 1).wait_recv()
-            to_y[k - 1] = part[k - 1, c] + from_sib[k - 1]
-            y_copy(k - 1, 0).start()
-
-        return carry
-
-    lax.fori_loop(0, 4, adjoint, 0)
+    quarter = pl.ds(pl.multiple_of(x * (NZ // 4), 8), NZ // 4)
+    for step in (1, 2, 3):
+        send(coil_maps.at[:, lax.rem(y + step, 4), :, quarter], maps.at[4 - step, c, :, :, quarter],
+             map_send, map_recv, at_y(step))
+    for k in range(3):
+        sib_copy(k).wait_recv()
+        to_y[k] = part[k, c] + from_sib[k]
+        y_copy(k, 0).start()
     for k in range(3):
         y_copy(k, 1).start()
-    for copy in map_copies:
-        copy.wait_recv()
+    send(own_maps.at[:, y], maps.at[0, c], map_sib_send.at[0], map_sib_recv.at[0], sibling)
     slots = maps.at[pl.ds(1, 3), c, :, :, quarter]
-    turns = [
-        send(slots, slots, turn_send.at[step - 1], turn_recv.at[step - 1], at_xz(step, 0, c))
-        for step in (1, 2, 3)
-    ]
+    arrived(slots, map_recv)
+    for step in (1, 2, 3):
+        send(slots, slots, turn_send, turn_recv, at_xz(step, 0, c))
     sib_copy(3).wait_recv()
+    part[3, c] = part[3, c] + from_sib[3]
     for h in range(2):
         at = half(h)
-        own = part[3, c, :, at] + from_sib[3, :, at]
-        for k in range(3):
-            y_copy(k, h).wait_recv()
-            own = own + from_y[k, :, at]
-        to_z[0, :, at] = own
+        arrived(from_y.at[:, :, at], y_recv.at[h])
+        to_z[0, :, at] = part[3, c, :, at] + from_y[0, :, at] + from_y[1, :, at] + from_y[2, :, at]
         z_copy(0, h).start()
-    for copy in turns:
-        copy.wait_recv()
-    slots = maps.at[pl.ds(1, 3), c]
-    sib_maps.append(send(slots, slots, map_sib_send.at[1], map_sib_recv.at[1], sibling))
+    turned = maps.at[pl.ds(1, 3), c, :, :, pl.ds(0, 3 * (NZ // 4))]
+    arrived(turned, turn_recv)
+    rest = maps.at[pl.ds(1, 3), c]
+    send(rest, rest, map_sib_send.at[1], map_sib_recv.at[1], sibling)
     slot_copy.wait()
     late_load.wait()
 
@@ -298,87 +295,88 @@
     lane = lax.broadcasted_iota(jnp.int32, (1, 128), 1)
 
     def share(which, stage, peers, me):
-        copies = [
+        for peer in peers:
             send(message.at[which, stage], sums.at[which, stage, me],
-                 sum_send.at[which, stage, n], sum_recv.at[which, stage, n], peer)
-            for n, peer in enumerate(peers)
-        ]
+                 sum_send.at[which, stage], sum_recv.at[which, stage], peer)
         sums[which, stage, me] = message[which, stage]
-        return copies
-
-    def collect(which, stage, copies):
-        for copy in copies:
-            copy.wait()
-        return jnp.sum(sums[which, stage, :len(copies) + 1], axis=0)
+
+    def collect(which, stage, peers):
+        lines = sums.at[which, stage, pl.ds(0, len(peers))]
+        arrived(lines, sum_recv.at[which, stage])
+        departed(lines, sum_send.at[which, stage])
+        return jnp.sum(sums[which, stage, :len(peers) + 1], axis=0)
+
+    def first_group(which):
+        if which == 2:
+            return near_peers, lax.rem(ring, 4) * 2 + c
+        return column_peers, ring * 2 + c
 
     def reduce_start(which, parts):
         line = jnp.zeros((1, 128), F32)
         for n, value in enumerate(parts):
             line = jnp.where(lane == n, total(value), line)
         message[which, 0] = line
-        peers, me = (image_peers, y * 2 + c) if which == 2 else (coil_peers, j)
-        return share(which, 0, peers, me)
-
-    def reduce_end(which, copies, count, meanwhile):
-        message[which, 1] = collect(which, 0, copies)
-        copies = share(which, 1, bin_peers, b)
+        share(which, 0, *first_group(which))
+
+    def reduce_end(which, count, meanwhile):
+        message[which, 1] = collect(which, 0, first_group(which)[0])
+        share(which, 1, plane_peers, y * 4 + x)
         meanwhile()
-        line = collect(which, 1, copies)
+        line = collect(which, 1, plane_peers)
         return [line[:, n:n + 1] for n in range(count)]
 
-    near, along, onward, far = [], [], [], []
-
-    def publish(n):
+    def publish(n, h):
+        lines = fields.at[n, 1 + c, y, :, half(h)]
+        for step in (1, 2, 3):
+            send(lines, lines, along_send.at[n], along_recv.at[n], at_y(step))
+
+    def near_copy(n, which):
         mine = fields.at[n, 1 + c, y]
-        near.append([
-            send(mine, mine, near_send.at[n, 0], near_recv.at[n, 0], sibling),
-            send(mine, fields.at[n, 3 - 3 * c, y], near_send.at[n, 1], near_recv.at[n, 1], across),
-        ])
-        along.append([
-            send(mine, mine, along_send.at[n, step - 1], along_recv.at[n, 4 - step - 1], at_y(step))
-            for step in (1, 2, 3)
-        ])
+        target, device = ((mine, sibling), (fields.at[n, 3 - 3 * c, y], across))[which]
+        return remote(mine, target, near_send.at[n, which], near_recv.at[n, which], device)
+
+    def announce(n):
+        near_copy(n, 0).start()
+        near_copy(n, 1).start()
+
+    def greet(n):
+        near_copy(n, 0).wait_recv()
+        near_copy(n, 1).wait_recv()
 
     def pass_on(n):
-        onward.append([])
-        for slot in (1, 3, 2):
-            along[n][3 - slot].wait_recv()
+        arrived(fields.at[n, 1 + c, pl.ds(0, 3)], along_recv.at[n])
+        for slot in (1, 2, 3):
             line = lax.rem(y + slot, 4)
             plane = fields.at[n, 1 + c, line]
-            onward[n] += [
-                send(plane, plane, pass_send.at[n, 0, slot - 1], pass_recv.at[n, 0, slot - 1], sibling),
-                send(plane, fields.at[n, 3 - 3 * c, line],
-                     pass_send.at[n, 1, slot - 1], pass_recv.at[n, 1, slot - 1], across),
-            ]
-
-    def greet(n):
-        for copy in near[n]:
-            copy.wait_recv()
+            send(plane, fields.at[n, 3 - 3 * c, line], pass_send.at[n, 1], pass_recv.at[n, 1], across)
+            send(plane, plane, pass_send.at[n, 0], pass_recv.at[n, 0], sibling)
+
+    def far_copy(n):
+        planes = fields.at[n, 3 * c]
+        return remote(planes, planes, far_send.at[n], far_recv.at[n], sibling)
 
     def hand_over(n):
-        for copy in onward[n][1::2]:
-            copy.wait_recv()
-        planes = fields.at[n, 3 * c]
-        far.append(send(planes, planes, far_send.at[n], far_recv.at[n], sibling))
+        arrived(fields.at[n, 3 * c, pl.ds(0, 3)], pass_recv.at[n, 1])
+        far_copy(n).start()
 
     def settle(n):
-        for copy in onward[n][::2]:
-            copy.wait_recv()
-        far[n].wait_recv()
+        arrived(fields.at[n, 2 - c, pl.ds(0, 3)], pass_recv.at[n, 0])
+        far_copy(n).wait_recv()
 
     zero = jnp.zeros((8, 128), F32)
-    for copy in sib_maps:
-        copy.wait_recv()
+    arrived(maps.at[0, c], map_sib_recv.at[0])
+    arrived(rest, map_sib_recv.at[1])
     for h in range(2):
         at = half(h)
         z_copy(0, h).wait_recv()
         rhs[:, at] = to_z[0, :, at] + from_z[0, :, at]
+        publish(0, h)
         spread(rhs, h)
-    publish(0)
+    announce(0)
     energy = lax.fori_loop(0, 4, normal, zero)
-    copies = reduce_start(0, [0.5 * inner(rhs, rhs), energy])
+    reduce_start(0, [0.5 * inner(rhs, rhs), energy])
     lax.fori_loop(0, 2, gather, 0)
-    norm_0, energy_0 = reduce_end(0, copies, 2, lambda: pass_on(0))
+    norm_0, energy_0 = reduce_end(0, 2, lambda: pass_on(0))
     curve_0 = energy_0 + 0.1 * norm_0
     alpha_0 = norm_0 / curve_0
     for h in range(2):
@@ -386,13 +384,15 @@
         z_copy(1, h).wait_recv()
         quad[:, at] = to_z[1, :, at] + from_z[1, :, at] + 0.1 * rhs[:, at]
         resid[:, at] = rhs[:, at] - alpha_0 * quad[:, at]
+        publish(1, h)
+        if h == 1:
+            announce(1)
         spread(resid, h)
-    publish(1)
     greet(0)
     hand_over(0)
     energy = lax.fori_loop(0, 4, forward, zero)
-    copies = reduce_start(1, [0.5 * inner(resid, resid), 0.5 * inner(resid, quad), energy])
-    norm_1, cross, energy_1 = reduce_end(1, copies, 3, lambda: pass_on(1))
+    reduce_start(1, [0.5 * inner(resid, resid), 0.5 * inner(resid, quad), energy])
+    norm_1, cross, energy_1 = reduce_end(1, 3, lambda: pass_on(1))
     beta = norm_1 / norm_0
     curve_1 = energy_1 + 0.1 * norm_1 + 2.0 * beta * cross + beta * beta * curve_0
     alpha_1 = norm_1 / curve_1
@@ -406,7 +406,7 @@
         return jnp.sqrt(gap[0] * gap[0] + gap[1] * gap[1])
 
     gap = jnp.where(2 * b + c < BINS - 1, iterate(2 + c, y) - iterate(1 + c, y), 0.0)
-    copies = reduce_start(2, [fold(length(gap))])
+    reduce_start(2, [fold(length(gap))])
 
     def differences(line, carry):
         values = [iterate(place, line) for place in range(4)]
@@ -417,7 +417,7 @@
             if keep is not None:
                 gap = jnp.where(keep, gap, 0.0)
             gaps[line, n] = gap
-            sizes[line, n] = length(gap)
+            sizes[line, n] = 1.0 / length(gap)
         return carry
 
     def prepare():
@@ -426,7 +426,7 @@
         settle(1)
         lax.fori_loop(0, SL, differences, 0)
 
-    (size_sum,) = reduce_end(2, copies, 1, prepare)
+    (size_sum,) = reduce_end(2, 1, prepare)
     lam = size_sum / COUNT + 1e-06
 
     def out_copy(line):
@@ -434,7 +434,7 @@
 
     def finish(line, carry):
         dual = [
-            gaps[line, n] * (lam / jnp.maximum(sizes[line, n], lam))[None] for n in range(3)
+            gaps[line, n] * jnp.minimum(lam * sizes[line, n], 1.0)[None] for n in range(3)
         ]
         for n in range(2):
             result[line, n] = result[line, n] + 0.25 * (dual[n + 1] - dual[n])
@@ -444,18 +444,20 @@
     lax.fori_loop(0, SL, finish, 0)
     for k in range(4):
         sib_copy(k).wait_send()
-    for k in range(3):
-        for h in range(2):
-            y_copy(k, h).wait_send()
-        map_copies[k].wait_send()
-        turns[k].wait_send()
+    departed(slots, map_send)
+    departed(turned, turn_send)
+    departed(maps.at[0, c], map_sib_send.at[0])
+    departed(rest, map_sib_send.at[1])
+    departed(to_y, y_send)
     for n in range(2):
         for h in range(2):
             z_copy(n, h).wait_send()
-        for copy in near[n] + along[n] + onward[n] + [far[n]]:
-            copy.wait_send()
-    for copy in sib_maps:
-        copy.wait_send()
+        near_copy(n, 0).wait_send()
+        near_copy(n, 1).wait_send()
+        departed(fields.at[n, 1 + c, pl.ds(0, 3)], along_send.at[n])
+        for which in range(2):
+            departed(fields.at[n, 1 + c, pl.ds(0, 3)], pass_send.at[n, which])
+        far_copy(n).wait_send()
     for line in range(SL):
         out_copy(line).wait()
 
@@ -493,11 +495,11 @@
             pltpu.VMEM((3, 2, 1, 128), F32),
             pltpu.VMEM((3, 2, 16, 1, 128), F32),
             dma((5,)), dma((4,)), dma(()),
-            dma((3,)), dma((3,)), dma((3,)), dma((3,)), dma((2,)), dma((2,)),
-            dma((4,)), dma((4,)), dma((3, 2)), dma((3, 2)), dma((2, 2)), dma((2, 2)),
-            dma((2, 2)), dma((2, 2)), dma((2, 3)), dma((2, 3)),
-            dma((2, 2, 3)), dma((2, 2, 3)), dma((2,)), dma((2,)),
-            dma((3, 2, 15)), dma((3, 2, 15)), dma((SL,)),
+            dma(()), dma(()), dma(()), dma(()), dma((2,)), dma((2,)),
+            dma((4,)), dma((4,)), dma(()), dma((2,)), dma((2, 2)), dma((2, 2)),
+            dma((2, 2)), dma((2, 2)), dma((2,)), dma((2,)),
+            dma((2, 2)), dma((2, 2)), dma((2,)), dma((2,)),
+            dma((3, 2)), dma((3, 2)), dma((SL,)),
         ],
         compiler_params=pltpu.CompilerParams(
             collective_id=0, has_side_effects=True, vmem_limit_bytes=60 * 1024 * 1024

time: 91.1 us -> 89.9 us (0.987)
  Pallas kernels: 88.3 us -> 87.1 us
    pallas_call x1, Pallas kernels: 88.3 us -> 87.1 us  [on_device(): pl.pallas_call(kernel, out_shape=jax.ShapeDtypeStruct((2, SL) + PLANE, F3...]
where the time goes in v4:
time: 89.9 us; the launch traced here: 89.8 us
  Pallas kernels  87.1 us (97%)
  local copies, waits for them, and re-layouts  2.69 us (3%)
    pallas_call x1, Pallas kernels, on_device(): pl.pallas_call(kernel, out_shape=jax.ShapeDtypeStruct((2, SL) + PLANE, F3...  87.1 us
    unnamed x1, local copies, waits for them, and re-layouts  2.69 us

profile of v4, /device:TPU:1, one launch (start us, length us, event | category | flops | bytes accessed | tf_op | source)
XLA Modules:
  0.0 89.8 jit_solution(2041950445982714750)
XLA Ops:
  0.0 87.1 %shard_map.55 = f32[2,4,2,96,256]{4,3,2,1,0:T(8,128)} custom-call(f32[2,2,4,2,96,256]{5,4,3,2,1,0:T(8,128)} %kspace.1, f32[2,4,2,96,256]{4,3,2,1,0:T(8,128)} %coil_maps.1, s32[2,96,256]{2,1,0:T(8,128)} %mask.1, bf16[2,2,512,512]{3,2,1,0:T(8,128)(2,1)} %constant.4.clone.row_table, bf16[2,2,192,192]{3,2,1,0:T(8,128)(2,1)} %constant.5.clone.col_table), custom_call_target="tpu_custom_call" | custom-call | flops 20000000000 | bytes 10000000 | tf_op jit(solution)/shard_map/pallas_call | solution.py:468
  87.1 2.7 %copy.7 = f32[2,4,2,96,256]{4,3,2,1,0:T(8,128)} copy(f32[2,4,2,96,256]{4,3,2,1,0:T(8,128)} %shard_map.55) | data formatting | bytes 3145728

commit v5 on v4

--- a/solution.py
+++ b/solution.py
@@ -17,6 +17,7 @@
 COUNT = (BINS - 1) * SL * NZ * NY
 PLANE = (2, NZ, NY)
 HALF = NZ // 2
+CHUNK = NZ // 4
 
 
 def dft_tables(length):
@@ -73,13 +74,13 @@
 
 def kernel(
     kspace, coil_maps, mask, row_table, col_table, out,
-    samples, own_maps, ticks, row, col, maps, weight, high, low, mid,
+    samples, own_maps, ticks, row, col, maps, weight, high, low, lines_high, lines_low, mid,
     part, from_sib, to_y, from_y, to_z, from_z,
     fields, quad, gaps, sizes, result, message, sums,
     load_sem, sample_sem, slot_sem,
     map_send, map_recv, turn_send, turn_recv, map_sib_send, map_sib_recv,
     sib_send, sib_recv, y_send, y_recv, z_send, z_recv,
-    near_send, near_recv, along_send, along_recv, pass_send, pass_recv, far_send, far_recv,
+    near_send, near_recv, along_send, along_recv, pass_send, pass_recv, far_send, far_recv, core_send, core_recv,
     sum_send, sum_recv, out_sem,
 ):
     b = lax.axis_index("bin")
@@ -162,14 +163,21 @@
     def sib_copy(k):
         return remote(part.at[k, 1 - c], from_sib.at[k], sib_send.at[k], sib_recv.at[k], sibling)
 
-    def y_copy(k, h):
+    def chunk(r):
+        return pl.ds(r * CHUNK, CHUNK)
+
+    def y_start(r):
+        for k in range(3):
+            send(to_y.at[k, :, chunk(r)], from_y.at[k, :, chunk(r)], y_send, y_recv.at[r], at_y(3 - k))
+
+    def first_z(r):
         return remote(
-            to_y.at[k, :, half(h)], from_y.at[k, :, half(h)], y_send, y_recv.at[h], at_y(3 - k)
+            to_z.at[0, :, chunk(r)], from_z.at[0, :, chunk(r)], z_send.at[0], z_recv.at[r], opposite
         )
 
-    def z_copy(n, h):
+    def second_z(h):
         return remote(
-            to_z.at[n, :, half(h)], from_z.at[n, :, half(h)], z_send.at[n, h], z_recv.at[n, h], opposite
+            to_z.at[1, :, half(h)], from_z.at[1, :, half(h)], z_send.at[1], z_recv.at[4 + h], opposite
         )
 
     def adjoint(k, carry):
@@ -180,14 +188,13 @@
             values = jnp.concatenate(
                 [samples[k, t // 2, t % 2, 0] * w, samples[k, t // 2, t % 2, 1] * w], axis=1
             )
-            high[0, t * NZ:(t + 1) * NZ], low[0, t * NZ:(t + 1) * NZ] = split(values)
-        used = pl.ds(0, 4 * NZ)
-        mid[0, used] = rows(high[0, used], low[0, used], row, 1)
+            lines_high[t * NZ:(t + 1) * NZ], lines_low[t * NZ:(t + 1) * NZ] = split(values)
+        mid[:4 * NZ] = rows(lines_high[...], lines_low[...], row, 1)
         for bin_ in range(2):
             sum_re, sum_im = 0.0, 0.0
             for coil in range(2):
                 at = pl.ds((bin_ * 2 + coil) * NZ, NZ)
-                wave = cols(jnp.concatenate([mid[0, at, :NY], mid[0, at, NY:]], axis=0), col, 1)
+                wave = cols(jnp.concatenate([mid[at, :NY], mid[at, NY:]], axis=0), col, 1)
                 sens_re, sens_im = own_maps[coil, s, 0], own_maps[coil, s, 1]
                 sum_re += sens_re * wave[:NZ] + sens_im * wave[NZ:]
                 sum_im += sens_re * wave[NZ:] - sens_im * wave[:NZ]
@@ -206,58 +213,65 @@
     for k in range(3):
         sib_copy(k).wait_recv()
         to_y[k] = part[k, c] + from_sib[k]
-        y_copy(k, 0).start()
-    for k in range(3):
-        y_copy(k, 1).start()
+    y_start(0)
+    y_start(1)
     send(own_maps.at[:, y], maps.at[0, c], map_sib_send.at[0], map_sib_recv.at[0], sibling)
     slots = maps.at[pl.ds(1, 3), c, :, :, quarter]
+    sib_copy(3).wait_recv()
+    part[3, c] = part[3, c] + from_sib[3]
     arrived(slots, map_recv)
     for step in (1, 2, 3):
         send(slots, slots, turn_send, turn_recv, at_xz(step, 0, c))
-    sib_copy(3).wait_recv()
-    part[3, c] = part[3, c] + from_sib[3]
-    for h in range(2):
-        at = half(h)
-        arrived(from_y.at[:, :, at], y_recv.at[h])
+    for r in range(4):
+        at = chunk(r)
+        arrived(from_y.at[:, :, at], y_recv.at[r])
+        if r < 2:
+            y_start(r + 2)
         to_z[0, :, at] = part[3, c, :, at] + from_y[0, :, at] + from_y[1, :, at] + from_y[2, :, at]
-        z_copy(0, h).start()
+        first_z(r).start()
     turned = maps.at[pl.ds(1, 3), c, :, :, pl.ds(0, 3 * (NZ // 4))]
-    arrived(turned, turn_recv)
     rest = maps.at[pl.ds(1, 3), c]
-    send(rest, rest, map_sib_send.at[1], map_sib_recv.at[1], sibling)
     slot_copy.wait()
     late_load.wait()
 
-    def spread(field, h):
-        at = half(h)
-        field_re, field_im = field[0, at], field[1, at]
-
-        def one(n, carry):
-            for t in range(4):
-                sens_re, sens_im = maps[n, t // 2, t % 2, 0, at], maps[n, t // 2, t % 2, 1, at]
-                values = jnp.concatenate(
-                    [sens_re * field_re - sens_im * field_im, sens_re * field_im + sens_im * field_re], axis=1
-                )
-                to = pl.ds(pl.multiple_of((n * 4 + t) * HALF, 16), HALF)
-                high[h, to], low[h, to] = split(values)
-            return carry
-
-        lax.fori_loop(0, 4, one, 0)
-        mid[h] = rows(high[h], low[h], row, 0)
-
-    def masked(n):
-        at = pl.ds(pl.multiple_of(n * HALF, 16), HALF)
-        values = cols(
-            jnp.concatenate([mid[0, at, :NY], mid[1, at, :NY], mid[0, at, NY:], mid[1, at, NY:]], axis=0), col, 0
-        )
+    def pair(n):
+        late = n - 2
+        slot = jnp.where(n < 2, 0, 1 + lax.rem(late + 3, 3))
+        flip = jnp.where(n < 2, n, jnp.where(late < 3, 0, 1))
+        return slot, lax.rem(c + flip, 2)
+
+    def spread(field, n):
+        for t in range(4):
+            slot, core = pair(2 * n + t // 2)
+            sens_re, sens_im = maps[slot, core, t % 2, 0], maps[slot, core, t % 2, 1]
+            values = jnp.concatenate(
+                [sens_re * field[0] - sens_im * field[1], sens_re * field[1] + sens_im * field[0]], axis=1
+            )
+            lines_high[t * NZ:(t + 1) * NZ], lines_low[t * NZ:(t + 1) * NZ] = split(values)
+        mid[:4 * NZ] = rows(lines_high[...], lines_low[...], row, 0)
+
+    def masked(t):
+        at = pl.ds(t * NZ, NZ)
+        values = cols(jnp.concatenate([mid[at, :NY], mid[at, NY:]], axis=0), col, 0)
         w = weight[c]
-        return values * jnp.concatenate([w, w], axis=0), at
+        return values * jnp.concatenate([w, w], axis=0)
 
     def normal(n, energy):
+        @pl.when(n == 1)
+        def _():
+            arrived(turned, turn_recv)
+            send(rest, rest, map_sib_send.at[1], map_sib_recv.at[1], sibling)
+
+        @pl.when(n == 2)
+        def _():
+            arrived(rest, map_sib_recv.at[1])
+
+        spread(rhs, n)
         for t in range(4):
-            values, at = masked(n * 4 + t)
+            values = masked(t)
             energy = energy + fold(values * values)
             wave = cols(values, col, 1)
+            at = pl.ds(pl.multiple_of((n * 4 + t) * HALF, 16), HALF)
             for h in range(2):
                 lines = jnp.concatenate(
                     [wave[h * HALF:(h + 1) * HALF], wave[NZ + h * HALF:NZ + (h + 1) * HALF]], axis=1
@@ -266,26 +280,28 @@
         return energy
 
     def gather(h, carry):
-        mid[h] = rows(high[h], low[h], row, 1)
+        mid[...] = rows(high[h], low[h], row, 1)
         at = half(h)
 
         def one(n, sums_):
             sum_re, sum_im = sums_
             for t in range(4):
                 lines = pl.ds(pl.multiple_of((n * 4 + t) * HALF, 16), HALF)
-                sens_re, sens_im = maps[n, t // 2, t % 2, 0, at], maps[n, t // 2, t % 2, 1, at]
-                sum_re += sens_re * mid[h, lines, :NY] + sens_im * mid[h, lines, NY:]
-                sum_im += sens_re * mid[h, lines, NY:] - sens_im * mid[h, lines, :NY]
+                slot, core = pair(2 * n + t // 2)
+                sens_re, sens_im = maps[slot, core, t % 2, 0, at], maps[slot, core, t % 2, 1, at]
+                sum_re += sens_re * mid[lines, :NY] + sens_im * mid[lines, NY:]
+                sum_im += sens_re * mid[lines, NY:] - sens_im * mid[lines, :NY]
             return sum_re, sum_im
 
         none = jnp.zeros((HALF, NY), F32)
         to_z[1, 0, at], to_z[1, 1, at] = lax.fori_loop(0, 4, one, (none, none))
-        z_copy(1, h).start()
+        second_z(h).start()
         return carry
 
     def forward(n, energy):
+        spread(resid, n)
         for t in range(4):
-            values, _ = masked(n * 4 + t)
+            values = masked(t)
             energy = energy + fold(values * values)
         return energy
 
@@ -339,65 +355,65 @@
         near_copy(n, 0).start()
         near_copy(n, 1).start()
 
-    def greet(n):
-        near_copy(n, 0).wait_recv()
+    def extend(n):
         near_copy(n, 1).wait_recv()
+        plane = fields.at[n, 3 * c, y]
+        for step in (1, 3):
+            send(plane, plane, far_send.at[n], far_recv.at[n], at_y(step))
 
     def pass_on(n):
         arrived(fields.at[n, 1 + c, pl.ds(0, 3)], along_recv.at[n])
+        facing = lax.rem(y + 2, 4)
+        plane = fields.at[n, 1 + c, facing]
+        send(plane, fields.at[n, 3 - 3 * c, facing], pass_send.at[n], pass_recv.at[n], across)
         for slot in (1, 2, 3):
-            line = lax.rem(y + slot, 4)
-            plane = fields.at[n, 1 + c, line]
-            send(plane, fields.at[n, 3 - 3 * c, line], pass_send.at[n, 1], pass_recv.at[n, 1], across)
-            send(plane, plane, pass_send.at[n, 0], pass_recv.at[n, 0], sibling)
-
-    def far_copy(n):
+            plane = fields.at[n, 1 + c, lax.rem(y + slot, 4)]
+            send(plane, plane, core_send.at[n, 0], core_recv.at[n, 0], sibling)
+
+    def hand_over(n):
+        arrived(fields.at[n, 3 * c, pl.ds(0, 2)], far_recv.at[n])
+        arrived(fields.at[n, 3 * c, 0], pass_recv.at[n])
         planes = fields.at[n, 3 * c]
-        return remote(planes, planes, far_send.at[n], far_recv.at[n], sibling)
-
-    def hand_over(n):
-        arrived(fields.at[n, 3 * c, pl.ds(0, 3)], pass_recv.at[n, 1])
-        far_copy(n).start()
+        send(planes, planes, core_send.at[n, 1], core_recv.at[n, 1], sibling)
 
     def settle(n):
-        arrived(fields.at[n, 2 - c, pl.ds(0, 3)], pass_recv.at[n, 0])
-        far_copy(n).wait_recv()
+        arrived(fields.at[n, 2 - c, pl.ds(0, 3)], core_recv.at[n, 0])
+        arrived(fields.at[n, 3 - 3 * c], core_recv.at[n, 1])
 
     zero = jnp.zeros((8, 128), F32)
     arrived(maps.at[0, c], map_sib_recv.at[0])
-    arrived(rest, map_sib_recv.at[1])
-    for h in range(2):
-        at = half(h)
-        z_copy(0, h).wait_recv()
+    for r in range(4):
+        at = chunk(r)
+        first_z(r).wait_recv()
         rhs[:, at] = to_z[0, :, at] + from_z[0, :, at]
-        publish(0, h)
-        spread(rhs, h)
+        if r % 2 == 1:
+            publish(0, r // 2)
     announce(0)
     energy = lax.fori_loop(0, 4, normal, zero)
     reduce_start(0, [0.5 * inner(rhs, rhs), energy])
+    extend(0)
     lax.fori_loop(0, 2, gather, 0)
     norm_0, energy_0 = reduce_end(0, 2, lambda: pass_on(0))
     curve_0 = energy_0 + 0.1 * norm_0
     alpha_0 = norm_0 / curve_0
     for h in range(2):
         at = half(h)
-        z_copy(1, h).wait_recv()
+        second_z(h).wait_recv()
         quad[:, at] = to_z[1, :, at] + from_z[1, :, at] + 0.1 * rhs[:, at]
         resid[:, at] = rhs[:, at] - alpha_0 * quad[:, at]
         publish(1, h)
-        if h == 1:
-            announce(1)
-        spread(resid, h)
-    greet(0)
+    announce(1)
+    near_copy(0, 0).wait_recv()
     hand_over(0)
     energy = lax.fori_loop(0, 4, forward, zero)
     reduce_start(1, [0.5 * inner(resid, resid), 0.5 * inner(resid, quad), energy])
+    extend(1)
     norm_1, cross, energy_1 = reduce_end(1, 3, lambda: pass_on(1))
     beta = norm_1 / norm_0
     curve_1 = energy_1 + 0.1 * norm_1 + 2.0 * beta * cross + beta * beta * curve_0
     alpha_1 = norm_1 / curve_1
     on_rhs = alpha_0 + alpha_1 * beta
-    greet(1)
+    near_copy(1, 0).wait_recv()
 
     def iterate(place, line):
         return on_rhs * fields[0, place, line] + alpha_1 * fields[1, place, line]
@@ -450,14 +466,14 @@
     departed(rest, map_sib_send.at[1])
     departed(to_y, y_send)
     for n in range(2):
-        for h in range(2):
-            z_copy(n, h).wait_send()
+        departed(to_z.at[n], z_send.at[n])
         near_copy(n, 0).wait_send()
         near_copy(n, 1).wait_send()
         departed(fields.at[n, 1 + c, pl.ds(0, 3)], along_send.at[n])
-        for which in range(2):
-            departed(fields.at[n, 1 + c, pl.ds(0, 3)], pass_send.at[n, which])
-        far_copy(n).wait_send()
+        departed(fields.at[n, 3 * c, pl.ds(0, 2)], far_send.at[n])
+        departed(fields.at[n, 1 + c, 0], pass_send.at[n])
+        departed(fields.at[n, 1 + c, pl.ds(0, 3)], core_send.at[n, 0])
+        departed(fields.at[n, 3 * c], core_send.at[n, 1])
     for line in range(SL):
         out_copy(line).wait()
 
@@ -480,7 +496,9 @@
             pltpu.VMEM(PLANE, F32),
             pltpu.VMEM((2, 16 * HALF, 2 * NY), BF16),
             pltpu.VMEM((2, 16 * HALF, 2 * NY), BF16),
-            pltpu.VMEM((2, 16 * HALF, 2 * NY), F32),
+            pltpu.VMEM((4 * NZ, 2 * NY), BF16),
+            pltpu.VMEM((4 * NZ, 2 * NY), BF16),
+            pltpu.VMEM((16 * HALF, 2 * NY), F32),
             pltpu.VMEM((4, 2) + PLANE, F32),
             pltpu.VMEM((4,) + PLANE, F32),
             pltpu.VMEM((3,) + PLANE, F32),
@@ -496,9 +514,9 @@
             pltpu.VMEM((3, 2, 16, 1, 128), F32),
             dma((5,)), dma((4,)), dma(()),
             dma(()), dma(()), dma(()), dma(()), dma((2,)), dma((2,)),
-            dma((4,)), dma((4,)), dma(()), dma((2,)), dma((2, 2)), dma((2, 2)),
+            dma((4,)), dma((4,)), dma(()), dma((4,)), dma((2,)), dma((6,)),
             dma((2, 2)), dma((2, 2)), dma((2,)), dma((2,)),
-            dma((2, 2)), dma((2, 2)), dma((2,)), dma((2,)),
+            dma((2,)), dma((2,)), dma((2,)), dma((2,)), dma((2, 2)), dma((2, 2)),
             dma((3, 2)), dma((3, 2)), dma((SL,)),
         ],
         compiler_params=pltpu.CompilerParams(

time: 89.9 us -> 87.7 us (0.976)
  Pallas kernels: 87.1 us -> 84.9 us
    pallas_call x1, Pallas kernels: 87.1 us -> 84.9 us  [on_device(): pl.pallas_call(kernel, out_shape=jax.ShapeDtypeStruct((2, SL) + PLANE, F3...]
where the time goes in v5:
time: 87.7 us; the launch traced here: 87.6 us
  Pallas kernels  84.9 us (97%)
  local copies, waits for them, and re-layouts  2.69 us (3%)
    pallas_call x1, Pallas kernels, on_device(): pl.pallas_call(kernel, out_shape=jax.ShapeDtypeStruct((2, SL) + PLANE, F3...  84.9 us
    unnamed x1, local copies, waits for them, and re-layouts  2.69 us

profile of v5, /device:TPU:1, one launch (start us, length us, event | category | flops | bytes accessed | tf_op | source)
XLA Modules:
  0.0 87.6 jit_solution(6999189755388563587)
XLA Ops:
  0.0 84.9 %shard_map.55 = f32[2,4,2,96,256]{4,3,2,1,0:T(8,128)} custom-call(f32[2,2,4,2,96,256]{5,4,3,2,1,0:T(8,128)} %kspace.1, f32[2,4,2,96,256]{4,3,2,1,0:T(8,128)} %coil_maps.1, s32[2,96,256]{2,1,0:T(8,128)} %mask.1, bf16[2,2,512,512]{3,2,1,0:T(8,128)(2,1)} %constant.4.clone.row_table, bf16[2,2,192,192]{3,2,1,0:T(8,128)(2,1)} %constant.5.clone.col_table), custom_call_target="tpu_custom_call" | custom-call | flops 20000000000 | bytes 10000000 | tf_op jit(solution)/shard_map/pallas_call | solution.py:484
  85.0 2.7 %copy.7 = f32[2,4,2,96,256]{4,3,2,1,0:T(8,128)} copy(f32[2,4,2,96,256]{4,3,2,1,0:T(8,128)} %shard_map.55) | data formatting | bytes 3145728

commit v6 on v5

--- a/solution.py
+++ b/solution.py
@@ -17,7 +17,8 @@
 COUNT = (BINS - 1) * SL * NZ * NY
 PLANE = (2, NZ, NY)
 HALF = NZ // 2
-CHUNK = NZ // 4
+EDGES = (0, 8, 24, 40, 56, 72, 88, 96)
+CHUNKS = len(EDGES) - 1
 
 
 def dft_tables(length):
@@ -35,14 +36,35 @@
 
 def row_tables():
     cos, sin = dft_tables(NY)
-    forward = np.block([[cos, -sin], [sin, cos]])
-    return np.stack([halves(forward), halves(forward.T)])
+    return halves(np.block([[cos, sin], [-sin, cos]]))
+
+
+def stacked(table, axis):
+    high, low = halves(table)
+    return np.concatenate([high, high, low], axis=axis)
+
+
+def parity_tables():
+    cos, sin = dft_tables(NY)
+    tables = []
+    for parity in range(2):
+        part = (slice(0, NY // 2), slice(parity, None, 2))
+        tables.append(np.block([[cos[part], -sin[part]], [sin[part], cos[part]]]))
+    return np.stack([
+        np.stack([stacked(table, 0) for table in tables]),
+        np.stack([stacked(table.T, 0) for table in tables]),
+    ])
 
 
 def col_tables():
     cos, sin = dft_tables(NZ)
     forward = np.block([[cos, sin], [-sin, cos]])
-    return np.stack([halves(forward), halves(forward.T)])
+    return np.stack([stacked(forward, 1), stacked(forward.T, 1)])
+
+
+def parity_order():
+    order = np.concatenate([np.arange(0, NY, 2), np.arange(1, NY, 2)])
+    return np.eye(NY)[:, order].astype(jnp.bfloat16)
 
 
 def split(values):
@@ -50,17 +72,28 @@
     return high, (values - high.astype(F32)).astype(BF16)
 
 
+def widened(values, axis):
+    high, low = split(values)
+    return jnp.concatenate([high, low, high], axis=axis)
+
+
 def dot(left, right):
     return jnp.dot(left, right, preferred_element_type=F32)
 
 
-def rows(high, low, table, which):
-    return dot(high, table[which, 0]) + dot(low, table[which, 0]) + dot(high, table[which, 1])
+def rows(high, low, table):
+    return dot(high, table[0]) + dot(low, table[0]) + dot(high, table[1])
 
 
 def cols(values, table, which):
-    high, low = split(values)
-    return dot(table[which, 0], high) + dot(table[which, 0], low) + dot(table[which, 1], high)
+    return dot(table[which], widened(values, 0))
+
+
+def by_parity(real, imag):
+    return [
+        jnp.concatenate([real[:, part], imag[:, part]], axis=1)
+        for part in (slice(0, NY // 2), slice(NY // 2, NY))
+    ]
 
 
 def fold(values):
@@ -73,8 +106,8 @@
 
 
 def kernel(
-    kspace, coil_maps, mask, row_table, col_table, out,
-    samples, own_maps, ticks, row, col, maps, weight, high, low, lines_high, lines_low, mid,
+    kspace, coil_maps, mask, row_table, col_table, parity_table, order_table, out,
+    samples, own_maps, ticks, row, col, half_row, order, maps, weight, lines_high, lines_low, first, lines, wide, mid,
     part, from_sib, to_y, from_y, to_z, from_z,
     fields, quad, gaps, sizes, result, message, sums,
     load_sem, sample_sem, slot_sem,
@@ -144,18 +177,19 @@
     greeted = column_peers + plane_peers + [across]
     for device in greeted:
         pl.semaphore_signal(barrier, inc=1, device_id=device, device_id_type=MESH)
-    loads = [load(mask, ticks, load_sem.at[0]), load(row_table.at[1], row.at[1], load_sem.at[1])]
+    loads = [load(mask, ticks, load_sem.at[0]), load(row_table, row, load_sem.at[1])]
     sample_copy(0).start()
-    loads += [load(col_table, col, load_sem.at[2]), load(coil_maps, own_maps, load_sem.at[3])]
+    loads += [load(col_table, col, load_sem.at[2]), load(coil_maps, own_maps, load_sem.at[3]), load(order_table, order, load_sem.at[5])]
     for k in (1, 2, 3):
         sample_copy(k).start()
-    late_load = load(row_table.at[0], row.at[0], load_sem.at[4])
+    late_load = load(parity_table, half_row, load_sem.at[4])
     slot_copy = load(coil_maps.at[:, y], maps.at[0, c], slot_sem)
     loads[0].wait()
     weight[0] = ticks[0].astype(F32)
     weight[1] = ticks[1].astype(F32)
     for copy in loads[1:]:
         copy.wait()
+    weight[2] = dot(weight[c].astype(BF16), order[...])
 
     def half(h):
         return pl.ds(pl.multiple_of(h * HALF, 16), HALF)
@@ -164,7 +198,7 @@
         return remote(part.at[k, 1 - c], from_sib.at[k], sib_send.at[k], sib_recv.at[k], sibling)
 
     def chunk(r):
-        return pl.ds(r * CHUNK, CHUNK)
+        return pl.ds(EDGES[r], EDGES[r + 1] - EDGES[r])
 
     def y_start(r):
         for k in range(3):
@@ -177,7 +211,7 @@
 
     def second_z(h):
         return remote(
-            to_z.at[1, :, half(h)], from_z.at[1, :, half(h)], z_send.at[1], z_recv.at[4 + h], opposite
+            to_z.at[1, :, half(h)], from_z.at[1, :, half(h)], z_send.at[1], z_recv.at[CHUNKS + h], opposite
         )
 
     def adjoint(k, carry):
@@ -189,12 +223,12 @@
                 [samples[k, t // 2, t % 2, 0] * w, samples[k, t // 2, t % 2, 1] * w], axis=1
             )
             lines_high[t * NZ:(t + 1) * NZ], lines_low[t * NZ:(t + 1) * NZ] = split(values)
-        mid[:4 * NZ] = rows(lines_high[...], lines_low[...], row, 1)
+        first[...] = rows(lines_high[...], lines_low[...], row)
         for bin_ in range(2):
             sum_re, sum_im = 0.0, 0.0
             for coil in range(2):
                 at = pl.ds((bin_ * 2 + coil) * NZ, NZ)
-                wave = cols(jnp.concatenate([mid[at, :NY], mid[at, NY:]], axis=0), col, 1)
+                wave = cols(jnp.concatenate([first[at, :NY], first[at, NY:]], axis=0), col, 1)
                 sens_re, sens_im = own_maps[coil, s, 0], own_maps[coil, s, 1]
                 sum_re += sens_re * wave[:NZ] + sens_im * wave[NZ:]
                 sum_im += sens_re * wave[NZ:] - sens_im * wave[:NZ]
@@ -222,10 +256,10 @@
     arrived(slots, map_recv)
     for step in (1, 2, 3):
         send(slots, slots, turn_send, turn_recv, at_xz(step, 0, c))
-    for r in range(4):
+    for r in range(CHUNKS):
         at = chunk(r)
         arrived(from_y.at[:, :, at], y_recv.at[r])
-        if r < 2:
+        if r + 2 < CHUNKS:
             y_start(r + 2)
         to_z[0, :, at] = part[3, c, :, at] + from_y[0, :, at] + from_y[1, :, at] + from_y[2, :, at]
         first_z(r).start()
@@ -244,17 +278,23 @@
         for t in range(4):
             slot, core = pair(2 * n + t // 2)
             sens_re, sens_im = maps[slot, core, t % 2, 0], maps[slot, core, t % 2, 1]
-            values = jnp.concatenate(
-                [sens_re * field[0] - sens_im * field[1], sens_re * field[1] + sens_im * field[0]], axis=1
+            left, right = by_parity(
+                sens_re * field[0] - sens_im * field[1], sens_re * field[1] + sens_im * field[0]
             )
-            lines_high[t * NZ:(t + 1) * NZ], lines_low[t * NZ:(t + 1) * NZ] = split(values)
-        mid[:4 * NZ] = rows(lines_high[...], lines_low[...], row, 0)
+            lines[0, t * NZ:(t + 1) * NZ] = widened(left + right, 1)
+            lines[1, t * NZ:(t + 1) * NZ] = widened(left - right, 1)
+        for parity in range(2):
+            mid[parity, :4 * NZ] = dot(lines[parity], half_row[0, parity])
 
     def masked(t):
         at = pl.ds(t * NZ, NZ)
-        values = cols(jnp.concatenate([mid[at, :NY], mid[at, NY:]], axis=0), col, 0)
-        w = weight[c]
-        return values * jnp.concatenate([w, w], axis=0)
+        even, odd = mid[0, at], mid[1, at]
+        mirror = jnp.concatenate([
+            jnp.concatenate([even[:, :NY // 2], odd[:, :NY // 2]], axis=1),
+            jnp.concatenate([even[:, NY // 2:], odd[:, NY // 2:]], axis=1),
+        ], axis=0)
+        w = weight[2]
+        return cols(mirror, col, 0) * jnp.concatenate([w, w], axis=0)
 
     def normal(n, energy):
         @pl.when(n == 1)
@@ -272,25 +312,28 @@
             energy = energy + fold(values * values)
             wave = cols(values, col, 1)
             at = pl.ds(pl.multiple_of((n * 4 + t) * HALF, 16), HALF)
-            for h in range(2):
-                lines = jnp.concatenate(
-                    [wave[h * HALF:(h + 1) * HALF], wave[NZ + h * HALF:NZ + (h + 1) * HALF]], axis=1
-                )
-                high[h, at], low[h, at] = split(lines)
+            for parity, part_ in enumerate(by_parity(wave[:NZ], wave[NZ:])):
+                for h in range(2):
+                    wide[h, parity, at] = widened(part_[h * HALF:(h + 1) * HALF], 1)
         return energy
 
     def gather(h, carry):
-        mid[...] = rows(high[h], low[h], row, 1)
+        for parity in range(2):
+            mid[parity] = dot(wide[h, parity], half_row[1, parity])
         at = half(h)
 
         def one(n, sums_):
             sum_re, sum_im = sums_
             for t in range(4):
-                lines = pl.ds(pl.multiple_of((n * 4 + t) * HALF, 16), HALF)
+                place = pl.ds(pl.multiple_of((n * 4 + t) * HALF, 16), HALF)
                 slot, core = pair(2 * n + t // 2)
                 sens_re, sens_im = maps[slot, core, t % 2, 0, at], maps[slot, core, t % 2, 1, at]
-                sum_re += sens_re * mid[lines, :NY] + sens_im * mid[lines, NY:]
-                sum_im += sens_re * mid[lines, NY:] - sens_im * mid[lines, :NY]
+                even, odd = mid[0, place], mid[1, place]
+                plus, minus = even + odd, even - odd
+                wave_re = jnp.concatenate([plus[:, :NY // 2], minus[:, :NY // 2]], axis=1)
+                wave_im = jnp.concatenate([plus[:, NY // 2:], minus[:, NY // 2:]], axis=1)
+                sum_re += sens_re * wave_re + sens_im * wave_im
+                sum_im += sens_re * wave_im - sens_im * wave_re
             return sum_re, sum_im
 
         none = jnp.zeros((HALF, NY), F32)
@@ -382,12 +425,13 @@
 
     zero = jnp.zeros((8, 128), F32)
     arrived(maps.at[0, c], map_sib_recv.at[0])
-    for r in range(4):
+    for r in range(CHUNKS):
         at = chunk(r)
         first_z(r).wait_recv()
         rhs[:, at] = to_z[0, :, at] + from_z[0, :, at]
-        if r % 2 == 1:
-            publish(0, r // 2)
+        if r == CHUNKS - 3:
+            publish(0, 0)
+    publish(0, 1)
     announce(0)
     energy = lax.fori_loop(0, 4, normal, zero)
     reduce_start(0, [0.5 * inner(rhs, rhs), energy])
@@ -484,21 +528,24 @@
     return pl.pallas_call(
         kernel,
         out_shape=jax.ShapeDtypeStruct((2, SL) + PLANE, F32),
-        in_specs=[whole] * 5,
+        in_specs=[whole] * 7,
         out_specs=whole,
         scratch_shapes=[
             pltpu.VMEM((4, 2, 2) + PLANE, F32),
             pltpu.VMEM((2, SL) + PLANE, F32),
             pltpu.VMEM(PLANE, jnp.int32),
-            pltpu.VMEM((2, 2, 2 * NY, 2 * NY), BF16),
-            pltpu.VMEM((2, 2, 2 * NZ, 2 * NZ), BF16),
+            pltpu.VMEM((2, 2 * NY, 2 * NY), BF16),
+            pltpu.VMEM((2, 2 * NZ, 6 * NZ), BF16),
+            pltpu.VMEM((2, 2, 3 * NY, NY), BF16),
+            pltpu.VMEM((NY, NY), BF16),
             pltpu.VMEM((4, 2, 2) + PLANE, F32),
-            pltpu.VMEM(PLANE, F32),
-            pltpu.VMEM((2, 16 * HALF, 2 * NY), BF16),
-            pltpu.VMEM((2, 16 * HALF, 2 * NY), BF16),
+            pltpu.VMEM((3, NZ, NY), F32),
             pltpu.VMEM((4 * NZ, 2 * NY), BF16),
             pltpu.VMEM((4 * NZ, 2 * NY), BF16),
-            pltpu.VMEM((16 * HALF, 2 * NY), F32),
+            pltpu.VMEM((4 * NZ, 2 * NY), F32),
+            pltpu.VMEM((2, 4 * NZ, 3 * NY), BF16),
+            pltpu.VMEM((2, 2, 16 * HALF, 3 * NY), BF16),
+            pltpu.VMEM((2, 16 * HALF, NY), F32),
             pltpu.VMEM((4, 2) + PLANE, F32),
             pltpu.VMEM((4,) + PLANE, F32),
             pltpu.VMEM((3,) + PLANE, F32),
@@ -512,9 +559,9 @@
             pltpu.VMEM((SL, 2) + PLANE, F32),
             pltpu.VMEM((3, 2, 1, 128), F32),
             pltpu.VMEM((3, 2, 16, 1, 128), F32),
-            dma((5,)), dma((4,)), dma(()),
+            dma((6,)), dma((4,)), dma(()),
             dma(()), dma(()), dma(()), dma(()), dma((2,)), dma((2,)),
-            dma((4,)), dma((4,)), dma(()), dma((4,)), dma((2,)), dma((6,)),
+            dma((4,)), dma((4,)), dma(()), dma((CHUNKS,)), dma((2,)), dma((CHUNKS + 2,)),
             dma((2, 2)), dma((2, 2)), dma((2,)), dma((2,)),
             dma((2,)), dma((2,)), dma((2,)), dma((2,)), dma((2, 2)), dma((2, 2)),
             dma((3, 2)), dma((3, 2)), dma((SL,)),
@@ -523,7 +570,10 @@
             collective_id=0, has_side_effects=True, vmem_limit_bytes=60 * 1024 * 1024
         ),
         cost_estimate=pl.CostEstimate(flops=20_000_000_000, bytes_accessed=10_000_000, transcendentals=0),
-    )(kspace, coil_maps, sample_mask, jnp.asarray(row_tables()), jnp.asarray(col_tables()))
+    )(
+        kspace, coil_maps, sample_mask, jnp.asarray(row_tables()), jnp.asarray(col_tables()),
+        jnp.asarray(parity_tables()), jnp.asarray(parity_order()),
+    )
 
 
 def solution(mesh):

time: 87.7 us -> 88 us (level)
  no operation moved by 1% of the time
where the time goes in v6:
time: 88 us; the launch traced here: 87.9 us
  Pallas kernels  85.2 us (97%)
  local copies, waits for them, and re-layouts  2.69 us (3%)
    pallas_call x1, Pallas kernels, on_device(): pl.pallas_call(kernel, out_shape=jax.ShapeDtypeStruct((2, SL) + PLANE, F3...  85.2 us
    unnamed x1, local copies, waits for them, and re-layouts  2.69 us

profile of v6, /device:TPU:1, one launch (start us, length us, event | category | flops | bytes accessed | tf_op | source)
XLA Modules:
  0.0 87.9 jit_solution(18162360637787580199)
XLA Ops:
  0.0 85.2 %shard_map.73 = f32[2,4,2,96,256]{4,3,2,1,0:T(8,128)} custom-call(f32[2,2,4,2,96,256]{5,4,3,2,1,0:T(8,128)} %kspace.1, f32[2,4,2,96,256]{4,3,2,1,0:T(8,128)} %coil_maps.1, s32[2,96,256]{2,1,0:T(8,128)} %mask.1, bf16[2,512,512]{2,1,0:T(8,128)(2,1)} %constant.8.clone.row_table, bf16[2,192,576]{2,1,0:T(8,128)(2,1)} %constant.9.clone.col_table, ...), custom_call_target="tpu_custom_call" | custom-call | flops 20000000000 | bytes 10000000 | tf_op jit(solution)/shard_map/pallas_call | solution.py:528
  85.2 2.7 %copy.9 = f32[2,4,2,96,256]{4,3,2,1,0:T(8,128)} copy(f32[2,4,2,96,256]{4,3,2,1,0:T(8,128)} %shard_map.73) | data formatting | bytes 3145728

commit v7 on v6

--- a/solution.py
+++ b/solution.py
@@ -17,7 +17,7 @@
 COUNT = (BINS - 1) * SL * NZ * NY
 PLANE = (2, NZ, NY)
 HALF = NZ // 2
-EDGES = (0, 8, 24, 40, 56, 72, 88, 96)
+EDGES = (0, 32, 64, 96)
 CHUNKS = len(EDGES) - 1
 
 
@@ -248,7 +248,6 @@
         sib_copy(k).wait_recv()
         to_y[k] = part[k, c] + from_sib[k]
     y_start(0)
-    y_start(1)
     send(own_maps.at[:, y], maps.at[0, c], map_sib_send.at[0], map_sib_recv.at[0], sibling)
     slots = maps.at[pl.ds(1, 3), c, :, :, quarter]
     sib_copy(3).wait_recv()
@@ -256,6 +255,7 @@
     arrived(slots, map_recv)
     for step in (1, 2, 3):
         send(slots, slots, turn_send, turn_recv, at_xz(step, 0, c))
+    y_start(1)
     for r in range(CHUNKS):
         at = chunk(r)
         arrived(from_y.at[:, :, at], y_recv.at[r])
@@ -296,9 +296,22 @@
         w = weight[2]
         return cols(mirror, col, 0) * jnp.concatenate([w, w], axis=0)
 
+    def publish(n):
+        plane = fields.at[n, 1 + c, y]
+        for step in (1, 2, 3):
+            send(plane, plane, along_send.at[n], along_recv.at[n], at_y(step))
+
+    def near_copy(n, which):
+        mine = fields.at[n, 1 + c, y]
+        target, device = ((mine, sibling), (fields.at[n, 3 - 3 * c, y], across))[which]
+        return remote(mine, target, near_send.at[n, which], near_recv.at[n, which], device)
+
     def normal(n, energy):
         @pl.when(n == 1)
         def _():
+            publish(0)
+            near_copy(0, 0).start()
+            near_copy(0, 1).start()
             arrived(turned, turn_recv)
             send(rest, rest, map_sib_send.at[1], map_sib_recv.at[1], sibling)
 
@@ -377,26 +390,13 @@
         message[which, 0] = line
         share(which, 0, *first_group(which))
 
-    def reduce_end(which, count, meanwhile):
+    def reduce_end(which, count, early, meanwhile):
+        early()
         message[which, 1] = collect(which, 0, first_group(which)[0])
         share(which, 1, plane_peers, y * 4 + x)
         meanwhile()
         line = collect(which, 1, plane_peers)
         return [line[:, n:n + 1] for n in range(count)]
-
-    def publish(n, h):
-        lines = fields.at[n, 1 + c, y, :, half(h)]
-        for step in (1, 2, 3):
-            send(lines, lines, along_send.at[n], along_recv.at[n], at_y(step))
-
-    def near_copy(n, which):
-        mine = fields.at[n, 1 + c, y]
-        target, device = ((mine, sibling), (fields.at[n, 3 - 3 * c, y], across))[which]
-        return remote(mine, target, near_send.at[n, which], near_recv.at[n, which], device)
-
-    def announce(n):
-        near_copy(n, 0).start()
-        near_copy(n, 1).start()
 
     def extend(n):
         near_copy(n, 1).wait_recv()
@@ -423,21 +423,30 @@
         arrived(fields.at[n, 2 - c, pl.ds(0, 3)], core_recv.at[n, 0])
         arrived(fields.at[n, 3 - 3 * c], core_recv.at[n, 1])
 
+    def idle():
+        pass
+
+    def first_window():
+        near_copy(1, 0).start()
+        near_copy(0, 0).wait_recv()
+        hand_over(0)
+
+    def second_window():
+        extend(1)
+        pass_on(1)
+
     zero = jnp.zeros((8, 128), F32)
     arrived(maps.at[0, c], map_sib_recv.at[0])
     for r in range(CHUNKS):
         at = chunk(r)
         first_z(r).wait_recv()
         rhs[:, at] = to_z[0, :, at] + from_z[0, :, at]
-        if r == CHUNKS - 3:
-            publish(0, 0)
-    publish(0, 1)
-    announce(0)
     energy = lax.fori_loop(0, 4, normal, zero)
     reduce_start(0, [0.5 * inner(rhs, rhs), energy])
+    lax.fori_loop(0, 2, gather, 0)
+    norm_0, energy_0 = reduce_end(0, 2, idle, idle)
     extend(0)
-    lax.fori_loop(0, 2, gather, 0)
-    norm_0, energy_0 = reduce_end(0, 2, lambda: pass_on(0))
+    pass_on(0)
     curve_0 = energy_0 + 0.1 * norm_0
     alpha_0 = norm_0 / curve_0
     for h in range(2):
@@ -445,14 +454,11 @@
         second_z(h).wait_recv()
         quad[:, at] = to_z[1, :, at] + from_z[1, :, at] + 0.1 * rhs[:, at]
         resid[:, at] = rhs[:, at] - alpha_0 * quad[:, at]
-        publish(1, h)
-    announce(1)
-    near_copy(0, 0).wait_recv()
-    hand_over(0)
+    publish(1)
+    near_copy(1, 1).start()
     energy = lax.fori_loop(0, 4, forward, zero)
     reduce_start(1, [0.5 * inner(resid, resid), 0.5 * inner(resid, quad), energy])
-    extend(1)
-    norm_1, cross, energy_1 = reduce_end(1, 3, lambda: pass_on(1))
+    norm_1, cross, energy_1 = reduce_end(1, 3, first_window, second_window)
     beta = norm_1 / norm_0
     curve_1 = energy_1 + 0.1 * norm_1 + 2.0 * beta * cross + beta * beta * curve_0
     alpha_1 = norm_1 / curve_1
@@ -481,12 +487,11 @@
         return carry
 
     def prepare():
-        hand_over(1)
         settle(0)
         settle(1)
         lax.fori_loop(0, SL, differences, 0)
 
-    (size_sum,) = reduce_end(2, 1, prepare)
+    (size_sum,) = reduce_end(2, 1, lambda: hand_over(1), prepare)
     lam = size_sum / COUNT + 1e-06
 
     def out_copy(line):

time: 88 us -> 83.3 us (0.947)
  Pallas kernels: 85.2 us -> 80.5 us
    pallas_call x1, Pallas kernels: 85.2 us -> 80.5 us  [on_device(): pl.pallas_call(kernel, out_shape=jax.ShapeDtypeStruct((2, SL) + PLANE, F3...]
where the time goes in v7:
time: 83.3 us; the launch traced here: 83.2 us
  Pallas kernels  80.5 us (97%)
  local copies, waits for them, and re-layouts  2.69 us (3%)
    pallas_call x1, Pallas kernels, on_device(): pl.pallas_call(kernel, out_shape=jax.ShapeDtypeStruct((2, SL) + PLANE, F3...  80.5 us
    unnamed x1, local copies, waits for them, and re-layouts  2.69 us

profile of v7, /device:TPU:1, one launch (start us, length us, event | category | flops | bytes accessed | tf_op | source)
XLA Modules:
  0.0 83.2 jit_solution(1930139060180981078)
XLA Ops:
  0.0 80.5 %shard_map.73 = f32[2,4,2,96,256]{4,3,2,1,0:T(8,128)} custom-call(f32[2,2,4,2,96,256]{5,4,3,2,1,0:T(8,128)} %kspace.1, f32[2,4,2,96,256]{4,3,2,1,0:T(8,128)} %coil_maps.1, s32[2,96,256]{2,1,0:T(8,128)} %mask.1, bf16[2,512,512]{2,1,0:T(8,128)(2,1)} %constant.8.clone.row_table, bf16[2,192,576]{2,1,0:T(8,128)(2,1)} %constant.9.clone.col_table, ...), custom_call_target="tpu_custom_call" | custom-call | flops 20000000000 | bytes 10000000 | tf_op jit(solution)/shard_map/pallas_call | solution.py:533
  80.5 2.7 %copy.9 = f32[2,4,2,96,256]{4,3,2,1,0:T(8,128)} copy(f32[2,4,2,96,256]{4,3,2,1,0:T(8,128)} %shard_map.73) | data formatting | bytes 3145728

commit v8 on v7

--- a/solution.py
+++ b/solution.py
@@ -19,6 +19,7 @@
 HALF = NZ // 2
 EDGES = (0, 32, 64, 96)
 CHUNKS = len(EDGES) - 1
+RING_HOPS = (0, 1, 2, 1)
 
 
 def dft_tables(length):
@@ -138,12 +139,13 @@
     opposite = (b, j + 2 - 4 * z)
     wraps = jnp.where(c == 1, jnp.where(x == 3, 1, 0), jnp.where(x == 0, -1, 0))
     across = at_xz(2 * c - 1, wraps, 1 - c)
-    column_peers = [at_xz(0, step // 2, lax.rem(c + step, 2)) for step in range(1, 16)]
-    near_peers = [
-        at_xz(0, dz, core) for dz in (0, 1, 2, -1) for core in (c, 1 - c)
-    ][1:]
+    column_peers = [
+        at_xz(0, dz, core) for dz in (4, 3, 5, 2, 6, 1, 7, 0) for core in (1 - c, c)
+    ][:-1]
+    near_peers = [at_xz(0, dz, core) for dz in (2, 1, -1, 0) for core in (1 - c, c)][:-1]
+    turns = sorted(range(1, 16), key=lambda step: -RING_HOPS[step % 4] - RING_HOPS[step // 4])
     plane_peers = [
-        (b - x + lax.rem(x + step % 4, 4), lax.rem(y + step // 4, 4) * 4 + z * 2 + c) for step in range(1, 16)
+        (b - x + lax.rem(x + step % 4, 4), lax.rem(y + step // 4, 4) * 4 + z * 2 + c) for step in turns
     ]
 
     def remote(source, target, send_sem, recv_sem, device):
@@ -442,8 +444,8 @@
         first_z(r).wait_recv()
         rhs[:, at] = to_z[0, :, at] + from_z[0, :, at]
     energy = lax.fori_loop(0, 4, normal, zero)
+    lax.fori_loop(0, 2, gather, 0)
     reduce_start(0, [0.5 * inner(rhs, rhs), energy])
-    lax.fori_loop(0, 2, gather, 0)
     norm_0, energy_0 = reduce_end(0, 2, idle, idle)
     extend(0)
     pass_on(0)

time: 83.3 us -> 91 us (1.092)
  Pallas kernels: 80.5 us -> 88.2 us
    pallas_call x1, Pallas kernels: 80.5 us -> 88.2 us  [on_device(): pl.pallas_call(kernel, out_shape=jax.ShapeDtypeStruct((2, SL) + PLANE, F3...]
where the time goes in v8:
time: 91 us; the launch traced here: 90.9 us
  Pallas kernels  88.2 us (97%)
  local copies, waits for them, and re-layouts  2.69 us (3%)
    pallas_call x1, Pallas kernels, on_device(): pl.pallas_call(kernel, out_shape=jax.ShapeDtypeStruct((2, SL) + PLANE, F3...  88.2 us
    unnamed x1, local copies, waits for them, and re-layouts  2.69 us

profile of v8, /device:TPU:1, one launch (start us, length us, event | category | flops | bytes accessed | tf_op | source)
XLA Modules:
  0.0 90.9 jit_solution(6700538875243250954)
XLA Ops:
  0.0 88.2 %shard_map.73 = f32[2,4,2,96,256]{4,3,2,1,0:T(8,128)} custom-call(f32[2,2,4,2,96,256]{5,4,3,2,1,0:T(8,128)} %kspace.1, f32[2,4,2,96,256]{4,3,2,1,0:T(8,128)} %coil_maps.1, s32[2,96,256]{2,1,0:T(8,128)} %mask.1, bf16[2,512,512]{2,1,0:T(8,128)(2,1)} %constant.8.clone.row_table, bf16[2,192,576]{2,1,0:T(8,128)(2,1)} %constant.9.clone.col_table, ...), custom_call_target="tpu_custom_call" | custom-call | flops 20000000000 | bytes 10000000 | tf_op jit(solution)/shard_map/pallas_call | solution.py:535
  88.2 2.7 %copy.9 = f32[2,4,2,96,256]{4,3,2,1,0:T(8,128)} copy(f32[2,4,2,96,256]{4,3,2,1,0:T(8,128)} %shard_map.73) | data formatting | bytes 3145728

commit v9 on v8

--- a/solution.py
+++ b/solution.py
@@ -444,8 +444,8 @@
         first_z(r).wait_recv()
         rhs[:, at] = to_z[0, :, at] + from_z[0, :, at]
     energy = lax.fori_loop(0, 4, normal, zero)
+    reduce_start(0, [0.5 * inner(rhs, rhs), energy])
     lax.fori_loop(0, 2, gather, 0)
-    reduce_start(0, [0.5 * inner(rhs, rhs), energy])
     norm_0, energy_0 = reduce_end(0, 2, idle, idle)
     extend(0)
     pass_on(0)

time: 91 us -> 83.2 us (0.914)
  Pallas kernels: 88.2 us -> 80.4 us
    pallas_call x1, Pallas kernels: 88.2 us -> 80.4 us  [on_device(): pl.pallas_call(kernel, out_shape=jax.ShapeDtypeStruct((2, SL) + PLANE, F3...]
where the time goes in v9:
time: 83.2 us; the launch traced here: 83.1 us
  Pallas kernels  80.4 us (97%)
  local copies, waits for them, and re-layouts  2.69 us (3%)
    pallas_call x1, Pallas kernels, on_device(): pl.pallas_call(kernel, out_shape=jax.ShapeDtypeStruct((2, SL) + PLANE, F3...  80.4 us
    unnamed x1, local copies, waits for them, and re-layouts  2.69 us

profile of v9, /device:TPU:1, one launch (start us, length us, event | category | flops | bytes accessed | tf_op | source)
XLA Modules:
  0.0 83.1 jit_solution(8244047319248676422)
XLA Ops:
  0.0 80.4 %shard_map.73 = f32[2,4,2,96,256]{4,3,2,1,0:T(8,128)} custom-call(f32[2,2,4,2,96,256]{5,4,3,2,1,0:T(8,128)} %kspace.1, f32[2,4,2,96,256]{4,3,2,1,0:T(8,128)} %coil_maps.1, s32[2,96,256]{2,1,0:T(8,128)} %mask.1, bf16[2,512,512]{2,1,0:T(8,128)(2,1)} %constant.8.clone.row_table, bf16[2,192,576]{2,1,0:T(8,128)(2,1)} %constant.9.clone.col_table, ...), custom_call_target="tpu_custom_call" | custom-call | flops 20000000000 | bytes 10000000 | tf_op jit(solution)/shard_map/pallas_call | solution.py:535
  80.4 2.7 %copy.9 = f32[2,4,2,96,256]{4,3,2,1,0:T(8,128)} copy(f32[2,4,2,96,256]{4,3,2,1,0:T(8,128)} %shard_map.73) | data formatting | bytes 3145728

commit v10 on v7

--- a/solution.py
+++ b/solution.py
@@ -107,7 +107,7 @@
 
 def kernel(
     kspace, coil_maps, mask, row_table, col_table, parity_table, order_table, out,
-    samples, own_maps, ticks, row, col, half_row, order, maps, weight, lines_high, lines_low, first, lines, wide, mid,
+    samples, own_maps, ticks, row, col, half_row, order, maps, weight, lines_high, lines_low, first, lines, spectra, wide, mid,
     part, from_sib, to_y, from_y, to_z, from_z,
     fields, quad, gaps, sizes, result, message, sums,
     load_sem, sample_sem, slot_sem,
@@ -323,12 +323,17 @@
         for t in range(4):
             values = masked(t)
             energy = energy + fold(values * values)
-            wave = cols(values, col, 1)
+            spectra[n * 4 + t] = values
+        return energy
+
+    def back(n, carry):
+        for t in range(4):
+            wave = cols(spectra[n * 4 + t], col, 1)
             at = pl.ds(pl.multiple_of((n * 4 + t) * HALF, 16), HALF)
             for parity, part_ in enumerate(by_parity(wave[:NZ], wave[NZ:])):
                 for h in range(2):
                     wide[h, parity, at] = widened(part_[h * HALF:(h + 1) * HALF], 1)
-        return energy
+        return carry
 
     def gather(h, carry):
         for parity in range(2):
@@ -443,6 +448,7 @@
         rhs[:, at] = to_z[0, :, at] + from_z[0, :, at]
     energy = lax.fori_loop(0, 4, normal, zero)
     reduce_start(0, [0.5 * inner(rhs, rhs), energy])
+    lax.fori_loop(0, 4, back, 0)
     lax.fori_loop(0, 2, gather, 0)
     norm_0, energy_0 = reduce_end(0, 2, idle, idle)
     extend(0)
@@ -549,6 +555,7 @@
             pltpu.VMEM((4 * NZ, 2 * NY), BF16),
             pltpu.VMEM((4 * NZ, 2 * NY), F32),
             pltpu.VMEM((2, 4 * NZ, 3 * NY), BF16),
+            pltpu.VMEM((16, 2 * NZ, NY), F32),
             pltpu.VMEM((2, 2, 16 * HALF, 3 * NY), BF16),
             pltpu.VMEM((2, 16 * HALF, NY), F32),
             pltpu.VMEM((4, 2) + PLANE, F32),

time: 83.3 us -> 83.7 us (level)
  no operation moved by 1% of the time
where the time goes in v10:
time: 83.7 us; the launch traced here: 83.6 us
  Pallas kernels  80.9 us (97%)
  local copies, waits for them, and re-layouts  2.69 us (3%)
    pallas_call x1, Pallas kernels, on_device(): pl.pallas_call(kernel, out_shape=jax.ShapeDtypeStruct((2, SL) + PLANE, F3...  80.9 us
    unnamed x1, local copies, waits for them, and re-layouts  2.69 us

profile of v10, /device:TPU:1, one launch (start us, length us, event | category | flops | bytes accessed | tf_op | source)
XLA Modules:
  0.0 83.6 jit_solution(1288114300061188305)
XLA Ops:
  0.0 80.9 %shard_map.73 = f32[2,4,2,96,256]{4,3,2,1,0:T(8,128)} custom-call(f32[2,2,4,2,96,256]{5,4,3,2,1,0:T(8,128)} %kspace.1, f32[2,4,2,96,256]{4,3,2,1,0:T(8,128)} %coil_maps.1, s32[2,96,256]{2,1,0:T(8,128)} %mask.1, bf16[2,512,512]{2,1,0:T(8,128)(2,1)} %constant.8.clone.row_table, bf16[2,192,576]{2,1,0:T(8,128)(2,1)} %constant.9.clone.col_table, ...), custom_call_target="tpu_custom_call" | custom-call | flops 20000000000 | bytes 10000000 | tf_op jit(solution)/shard_map/pallas_call | solution.py:539
  80.9 2.7 %copy.9 = f32[2,4,2,96,256]{4,3,2,1,0:T(8,128)} copy(f32[2,4,2,96,256]{4,3,2,1,0:T(8,128)} %shard_map.73) | data formatting | bytes 3145728

commit v11 on v7

--- a/solution.py
+++ b/solution.py
@@ -486,12 +486,36 @@
             sizes[line, n] = 1.0 / length(gap)
         return carry
 
+    def drain_first():
+        for k in range(4):
+            sib_copy(k).wait_send()
+        departed(slots, map_send)
+        departed(turned, turn_send)
+        departed(maps.at[0, c], map_sib_send.at[0])
+        departed(rest, map_sib_send.at[1])
+        departed(to_y, y_send)
+
+    def drain(n):
+        departed(to_z.at[n], z_send.at[n])
+        near_copy(n, 0).wait_send()
+        near_copy(n, 1).wait_send()
+        departed(fields.at[n, 1 + c, pl.ds(0, 3)], along_send.at[n])
+        departed(fields.at[n, 3 * c, pl.ds(0, 2)], far_send.at[n])
+        departed(fields.at[n, 1 + c, 0], pass_send.at[n])
+        departed(fields.at[n, 1 + c, pl.ds(0, 3)], core_send.at[n, 0])
+        departed(fields.at[n, 3 * c], core_send.at[n, 1])
+
+    def third_window():
+        hand_over(1)
+        drain_first()
+        drain(0)
+
     def prepare():
         settle(0)
         settle(1)
         lax.fori_loop(0, SL, differences, 0)
 
-    (size_sum,) = reduce_end(2, 1, lambda: hand_over(1), prepare)
+    (size_sum,) = reduce_end(2, 1, third_window, prepare)
     lam = size_sum / COUNT + 1e-06
 
     def out_copy(line):
@@ -507,22 +531,7 @@
         return carry
 
     lax.fori_loop(0, SL, finish, 0)
-    for k in range(4):
-        sib_copy(k).wait_send()
-    departed(slots, map_send)
-    departed(turned, turn_send)
-    departed(maps.at[0, c], map_sib_send.at[0])
-    departed(rest, map_sib_send.at[1])
-    departed(to_y, y_send)
-    for n in range(2):
-        departed(to_z.at[n], z_send.at[n])
-        near_copy(n, 0).wait_send()
-        near_copy(n, 1).wait_send()
-        departed(fields.at[n, 1 + c, pl.ds(0, 3)], along_send.at[n])
-        departed(fields.at[n, 3 * c, pl.ds(0, 2)], far_send.at[n])
-        departed(fields.at[n, 1 + c, 0], pass_send.at[n])
-        departed(fields.at[n, 1 + c, pl.ds(0, 3)], core_send.at[n, 0])
-        departed(fields.at[n, 3 * c], core_send.at[n, 1])
+    drain(1)
     for line in range(SL):
         out_copy(line).wait()
 

time: 83.3 us -> 83.3 us (level)
  no operation moved by 1% of the time
where the time goes in v11:
time: 83.3 us; the launch traced here: 83.2 us
  Pallas kernels  80.5 us (97%)
  local copies, waits for them, and re-layouts  2.69 us (3%)
    pallas_call x1, Pallas kernels, on_device(): pl.pallas_call(kernel, out_shape=jax.ShapeDtypeStruct((2, SL) + PLANE, F3...  80.5 us
    unnamed x1, local copies, waits for them, and re-layouts  2.69 us

profile of v11, /device:TPU:1, one launch (start us, length us, event | category | flops | bytes accessed | tf_op | source)
XLA Modules:
  0.0 83.2 jit_solution(5315281274988339126)
XLA Ops:
  0.0 80.5 %shard_map.73 = f32[2,4,2,96,256]{4,3,2,1,0:T(8,128)} custom-call(f32[2,2,4,2,96,256]{5,4,3,2,1,0:T(8,128)} %kspace.1, f32[2,4,2,96,256]{4,3,2,1,0:T(8,128)} %coil_maps.1, s32[2,96,256]{2,1,0:T(8,128)} %mask.1, bf16[2,512,512]{2,1,0:T(8,128)(2,1)} %constant.8.clone.row_table, bf16[2,192,576]{2,1,0:T(8,128)(2,1)} %constant.9.clone.col_table, ...), custom_call_target="tpu_custom_call" | custom-call | flops 20000000000 | bytes 10000000 | tf_op jit(solution)/shard_map/pallas_call | solution.py:542
  80.5 2.7 %copy.9 = f32[2,4,2,96,256]{4,3,2,1,0:T(8,128)} copy(f32[2,4,2,96,256]{4,3,2,1,0:T(8,128)} %shard_map.73) | data formatting | bytes 3145728
